TPU v7x, 32 devices: a whole 2x2x4 slice. The times are simulated.
32 devices in a mesh: layer: 8 (over z, y), rhs: 4 (over x, core).
Axes of the slice: x: 2, y: 2, z: 4, core: 2. Of those that a mesh axis runs over, the one named last changes fastest.
Arguments:
- coupling: float32 [8, 640, 640], P('layer', 'rhs'), may hold values from -8 to 12, as said below
- density: int32 [8, 640], P('layer'), may hold values 0 or 1
- support: float32 [8, 640], P('layer'), may hold values from 0.2 to 2
- loads: float32 [8, 640, 1024], P('layer', None, 'rhs'), may hold values from -6 to 6
Outputs:
- reduced_diag: float32 [8, 640, 640], P('layer', 'rhs')
- reduced_lower: float32 [8, 640, 640], P('layer', 'rhs')
- reduced_upper: float32 [8, 640, 640], P('layer', 'rhs')
- reduced_loads: float32 [8, 640, 1024], P('layer', None, 'rhs')
Inputs may be any that keep to these rules, and one draw needn't show every extreme that they name: Each coupling block is symmetric and positive definite.
All inputs are finite; a program needn't handle non-finite values. No bound on the sum of `density` on one device may be relied on, other than what follows from the above.
Results may differ from a plain program's by a relative error of at most 0.0003.
Values sent between devices are 32-bit elements; how exact they have to be, the bound alone decides.
A program may use at most 64 MiB of HBM per device.

v0:
```python
import jax
import jax.numpy as jnp
from jax import lax
from jax.sharding import PartitionSpec as P

LEVELS = 2


def from_behind(shard, axis, by):
    count = lax.axis_size(axis)
    pairs = [(i, i + by) for i in range(count) if 0 <= i + by < count]
    return lax.ppermute(shard, axis, pairs)


def solve_spd(factor, right):
    half = lax.linalg.triangular_solve(factor, right, left_side=True, lower=True)
    return lax.linalg.triangular_solve(factor, half, left_side=True, lower=True, transpose_a=True)


def solve_from_right(factor, left):
    half = lax.linalg.triangular_solve(factor, left, left_side=False, lower=True, transpose_a=True)
    return lax.linalg.triangular_solve(factor, half, left_side=False, lower=True)


def matmul(left, right):
    return jnp.dot(left, right, precision=lax.Precision.HIGHEST, preferred_element_type=jnp.float32)


def leading_matmul(left, right):
    return lax.dot_general(
        left,
        right,
        (((0,), (0,)), ((), ())),
        precision=lax.Precision.HIGHEST,
        preferred_element_type=jnp.float32,
    )


def shards(coupling, density, support, loads):
    ncols = coupling.shape[1]
    width = coupling.shape[2]
    column_part = lax.axis_index("rhs")
    layer_id = lax.axis_index("layer")
    last_layer = lax.axis_size("layer") - 1
    rho = 0.3 + 0.7 * density[0].astype(jnp.float32)
    rho_cols = lax.dynamic_slice_in_dim(rho, column_part * ncols, ncols, 0)
    stiff_t = rho_cols[:, None] * coupling[0] * rho[None, :]
    below_t = from_behind(stiff_t, "layer", 1)
    col_index = lax.broadcasted_iota(jnp.int32, (ncols, width), 0) + column_part * ncols
    row_index = lax.broadcasted_iota(jnp.int32, (ncols, width), 1)
    diag_part = jnp.where(row_index == col_index, support[0][None, :], jnp.float32(0.0))
    diag_t = below_t + stiff_t + diag_part
    lower_t = -below_t
    upper_t = jnp.where(layer_id < last_layer, -stiff_t, jnp.zeros_like(stiff_t))
    right = loads[0]
    for level in range(LEVELS):
        dist = 2**level
        full_diag_t, full_lower_t, full_upper_t = (
            lax.all_gather(diag_t, "rhs", axis=0, tiled=True),
            lax.all_gather(lower_t, "rhs", axis=0, tiled=True),
            lax.all_gather(upper_t, "rhs", axis=0, tiled=True),
        )
        factor = jnp.linalg.cholesky(full_diag_t.T)
        stacked = solve_from_right(factor, jnp.concatenate([lower_t, upper_t], axis=0))
        solved_lower = stacked[:ncols]
        solved_upper = stacked[ncols:]
        solved_right = solve_spd(factor, right)
        low_l, low_u, low_b = from_behind((solved_lower, solved_upper, solved_right), "layer", dist)
        high_l, high_u, high_b = from_behind(
            (solved_lower, solved_upper, solved_right), "layer", -dist
        )
        new_lower = -matmul(low_l, full_lower_t)
        new_upper = -matmul(high_u, full_upper_t)
        new_diag = diag_t - matmul(low_u, full_lower_t) - matmul(high_l, full_upper_t)
        new_right = (
            right - leading_matmul(full_lower_t, low_b) - leading_matmul(full_upper_t, high_b)
        )
        diag_t, lower_t, upper_t, right = (new_diag, new_lower, new_upper, new_right)
    return (diag_t[None], lower_t[None], upper_t[None], right[None])


def solution(mesh):
    placed = (P("layer", "rhs", None), P("layer", None), P("layer", None), P("layer", None, "rhs"))
    return jax.shard_map(
        shards,
        mesh=mesh,
        in_specs=placed,
        out_specs=(
            P("layer", "rhs", None),
            P("layer", "rhs", None),
            P("layer", "rhs", None),
            P("layer", None, "rhs"),
        ),
        check_vma=False,
    )
```

profile of v0, /device:TPU:0, one launch (start us, length us, event | category | flops | bytes accessed | tf_op | source)
XLA Modules:
  0.0 626.4 jit_solution(16977780586017470068)
XLA Ops:
  26.0 20.9 %all-gather.7.cloned.1.call-done = f32[640,640]{1,0:T(8,128)} async-done(((f32[160,640]{1,0:T(8,128)}), f32[640,640]{1,0:T(8,128)}) %all-gather.7.cloned.1.call-update) | async-done | bytes 1638416 | tf_op jit(solution)/shard_map/all_gather | solution.py:59
  50.4 11.7 %cholesky.364 = f32[128,128]{1,0:T(8,128)S(1)} custom-call(f32[128,128]{1,0:T(8,128)S(1)} %cholesky.542), custom_call_target="Cholesky" | custom-call | tf_op jit(solution)/shard_map/jit(cholesky)/cholesky | solution.py:63
  62.2 9.8 %custom-call.46 = f32[1,128,128]{1,2,0:T(8,128)S(1)} custom-call(f32[1,128,128]{2,1,0:T(8,128)S(1)} %get-tuple-element.126), custom_call_target="InvertDiagBlocksLowerTriangular" | custom-call | tf_op jit(solution)/shard_map/jit(cholesky)/cholesky | solution.py:63
  73.5 13.2 %cholesky.383 = f32[128,128]{1,0:T(8,128)} custom-call(f32[128,128]{1,0:T(8,128)} %cholesky.546), custom_call_target="Cholesky" | custom-call | tf_op jit(solution)/shard_map/jit(cholesky)/cholesky | solution.py:63
  88.2 20.0 %custom-call.47 = f32[1,128,128]{1,2,0:T(8,128)} custom-call(f32[1,128,128]{2,1,0:T(8,128)} %get-tuple-element.123), custom_call_target="InvertDiagBlocksLowerTriangular" | custom-call | tf_op jit(solution)/shard_map/jit(cholesky)/cholesky | solution.py:63
  109.9 12.3 %cholesky.404 = f32[128,128]{1,0:T(8,128)} custom-call(f32[128,128]{1,0:T(8,128)S(1)} %cholesky.551), custom_call_target="Cholesky" | custom-call | tf_op jit(solution)/shard_map/jit(cholesky)/cholesky | solution.py:63
  123.7 10.4 %custom-call.48 = f32[1,128,128]{1,2,0:T(8,128)} custom-call(f32[1,128,128]{2,1,0:T(8,128)S(1)} %get-tuple-element.120), custom_call_target="InvertDiagBlocksLowerTriangular" | custom-call | tf_op jit(solution)/shard_map/jit(cholesky)/cholesky | solution.py:63
  135.8 11.9 %cholesky.423 = f32[128,128]{1,0:T(8,128)S(1)} custom-call(f32[128,128]{1,0:T(8,128)S(1)} %cholesky.556), custom_call_target="Cholesky" | custom-call | tf_op jit(solution)/shard_map/jit(cholesky)/cholesky | solution.py:63
  158.8 11.7 %cholesky.440 = f32[128,128]{1,0:T(8,128)S(1)} custom-call(f32[128,128]{1,0:T(8,128)S(1)} %slice_subtract_fusion.15), custom_call_target="Cholesky" | custom-call | tf_op jit(solution)/shard_map/jit(cholesky)/cholesky | solution.py:63
  176.1 14.5 %while.16 = (s32[]{:T(128)}, f32[640,640]{1,0:T(8,128)}, s32[5,2]{0,1:T(2,128)S(1)}, f32[5,128,128]{2,1,0:T(8,128)S(1)}, s32[]{:T(128)}) while((s32[]{:T(128)}, f32[640,640]{1,0:T(8,128)}, s32[5,2]{0,1:T(2,128)S(1)}, f32[5,128,128]{2,1,0:T(8,128)S(1)}, s32[]{:T(128)}) %tuple.88), condition=%wide.while_cond, body=%wide.while_body.sunk | while | flops 2 | bytes 131181 | solution.py:21
  190.6 49.5 %custom-call.50 = f32[5,128,128]{1,2,0:T(8,128)S(1)} custom-call(f32[5,128,128]{2,1,0:T(8,128)S(1)} %get-tuple-element.65), custom_call_target="InvertDiagBlocksLowerTriangular" | custom-call | tf_op jit(solution)/shard_map/triangular_solve/custom-call.4 | solution.py:21
  262.5 13.1 %collective-permute-done.2 = f32[160,640]{1,0:T(8,128)} collective-permute-done((f32[160,640]{1,0:T(8,128)}, f32[160,640]{1,0:T(8,128)}, u32[]{:S(2)}, u32[]{:S(2)}) %collective-permute-start.2) | collective-permute-done | bytes 409632 | tf_op jit(solution)/shard_map/ppermute | solution.py:12
  325.4 11.4 %collective-permute-done.9 = f32[640,256]{1,0:T(8,128)} collective-permute-done((f32[640,256]{1,0:T(8,128)}, f32[640,256]{1,0:T(8,128)}, u32[]{:S(2)}, u32[]{:S(2)}) %collective-permute-start.9) | collective-permute-done | bytes 655392 | tf_op jit(solution)/shard_map/ppermute | solution.py:12
  345.5 11.7 %cholesky.455 = f32[128,128]{1,0:T(8,128)S(1)} custom-call(f32[128,128]{1,0:T(8,128)S(1)} %cholesky.560), custom_call_target="Cholesky" | custom-call | tf_op jit(solution)/shard_map/jit(cholesky)/cholesky | solution.py:63
  357.4 9.8 %custom-call.52 = f32[1,128,128]{1,2,0:T(8,128)S(1)} custom-call(f32[1,128,128]{2,1,0:T(8,128)S(1)} %get-tuple-element.113), custom_call_target="InvertDiagBlocksLowerTriangular" | custom-call | tf_op jit(solution)/shard_map/jit(cholesky)/cholesky | solution.py:63
  368.6 13.2 %cholesky.474 = f32[128,128]{1,0:T(8,128)} custom-call(f32[128,128]{1,0:T(8,128)} %cholesky.564), custom_call_target="Cholesky" | custom-call | tf_op jit(solution)/shard_map/jit(cholesky)/cholesky | solution.py:63
  384.6 11.4 %custom-call.53 = f32[1,128,128]{1,2,0:T(8,128)} custom-call(f32[1,128,128]{2,1,0:T(8,128)} %get-tuple-element.110), custom_call_target="InvertDiagBlocksLowerTriangular" | custom-call | tf_op jit(solution)/shard_map/jit(cholesky)/cholesky | solution.py:63
  397.6 12.3 %cholesky.495 = f32[128,128]{1,0:T(8,128)} custom-call(f32[128,128]{1,0:T(8,128)S(1)} %cholesky.569), custom_call_target="Cholesky" | custom-call | tf_op jit(solution)/shard_map/jit(cholesky)/cholesky | solution.py:63
  411.5 10.4 %custom-call.54 = f32[1,128,128]{1,2,0:T(8,128)} custom-call(f32[1,128,128]{2,1,0:T(8,128)S(1)} %get-tuple-element.107), custom_call_target="InvertDiagBlocksLowerTriangular" | custom-call | tf_op jit(solution)/shard_map/jit(cholesky)/cholesky | solution.py:63
  423.5 11.9 %cholesky.514 = f32[128,128]{1,0:T(8,128)S(1)} custom-call(f32[128,128]{1,0:T(8,128)S(1)} %cholesky.574), custom_call_target="Cholesky" | custom-call | tf_op jit(solution)/shard_map/jit(cholesky)/cholesky | solution.py:63
  446.5 11.7 %cholesky.531 = f32[128,128]{1,0:T(8,128)S(1)} custom-call(f32[128,128]{1,0:T(8,128)S(1)} %slice_subtract_fusion.14), custom_call_target="Cholesky" | custom-call | tf_op jit(solution)/shard_map/jit(cholesky)/cholesky | solution.py:63
  464.2 17.0 %while.17 = (s32[]{:T(128)}, f32[640,640]{1,0:T(8,128)}, s32[5,2]{0,1:T(2,128)S(1)}, f32[5,128,128]{2,1,0:T(8,128)}, s32[]{:T(128)}) while((s32[]{:T(128)}, f32[640,640]{1,0:T(8,128)}, s32[5,2]{0,1:T(2,128)S(1)}, f32[5,128,128]{2,1,0:T(8,128)}, s32[]{:T(128)}) %tuple.106), condition=%wide.while_cond.clone, body=%wide.while_body.clone.sunk | while | flops 2 | bytes 132705 | solution.py:21
  481.2 50.5 %custom-call.56 = f32[5,128,128]{1,2,0:T(8,128)S(1)} custom-call(f32[5,128,128]{2,1,0:T(8,128)} %get-tuple-element.67), custom_call_target="InvertDiagBlocksLowerTriangular" | custom-call | tf_op jit(solution)/shard_map/triangular_solve/custom-call.4 | solution.py:21
  554.0 23.1 %collective-permute-start.11 = (f32[640,256]{1,0:T(8,128)}, f32[640,256]{1,0:T(8,128)}, u32[]{:S(2)}, u32[]{:S(2)}) collective-permute-start(f32[640,256]{1,0:T(8,128)} %constant_dynamic-update-slice_fusion.12), channel_id=1, source_target_pairs={{0,8},{4,12},{8,16},{12,20},{16,24},{20,28},{1,9},{5,13},{9,17},{1... | collective-permute-start | bytes 1966088 | tf_op jit(solution)/shard_map/ppermute | solution.py:12
  (289 shorter events, 242.5 us)
Async XLA Ops:
  7.2 39.6 %all-gather.7.cloned.1.call-start = ((), (), s32[]{:S(2)}) async-start(), calls=%async_computation | async-start | bytes 2048000 | tf_op jit(solution)/shard_map/all_gather | solution.py:59
  9.9 13.6 %collective-permute-start = (f32[160,640]{1,0:T(8,128)S(1)}, f32[160,640]{1,0:T(8,128)S(1)}, u32[]{:S(2)}, u32[]{:S(2)}) collective-permute-start(f32[160,640]{1,0:T(8,128)S(1)} %get-tuple-element.90), channel_id=1, source_target_pairs={{0,4},{4,8},{8,12},{12,16},{16,20},{20,24},{24,28},{1,5},{5,9},{9,... | collective-permute-start | bytes 1228808 | tf_op jit(solution)/shard_map/ppermute | solution.py:12
  24.4 238.1 %all-gather.11.cloned.1.call-start = ((), (), s32[]{:S(2)}) async-start(), calls=%async_computation.2 | async-start | bytes 2048000 | tf_op jit(solution)/shard_map/all_gather | solution.py:61
  25.2 254.2 %all-gather.9.cloned.1.call-start = ((), (), s32[]{:S(2)}) async-start(), calls=%async_computation.1 | async-start | bytes 2048000 | tf_op jit(solution)/shard_map/all_gather | solution.py:60
  25.9 315.6 %all-gather.13.cloned.1.call-start = ((), (), s32[]{:S(2)}) async-start(), calls=%async_computation.3 | async-start | bytes 2048000 | tf_op jit(solution)/shard_map/all_gather | solution.py:59
  174.7 65.5 %copy-start.2 = (f32[160,640]{1,0:T(8,128)S(1)}, f32[160,640]{1,0:T(8,128)}, u32[]{:S(2)}) copy-start(f32[160,640]{1,0:T(8,128)} %get-tuple-element.89) | copy-start | bytes 1228804
  174.7 65.5 %copy-start.3 = (f32[160,640]{1,0:T(8,128)S(1)}, f32[160,640]{1,0:T(8,128)}, u32[]{:S(2)}) copy-start(f32[160,640]{1,0:T(8,128)} %get-tuple-element.100) | copy-start | bytes 1228804
  249.1 31.2 %collective-permute-start.1 = (f32[160,640]{1,0:T(8,128)}, f32[160,640]{1,0:T(8,128)}, u32[]{:S(2)}, u32[]{:S(2)}) collective-permute-start(f32[160,640]{1,0:T(8,128)} %get-tuple-element.97), channel_id=1, source_target_pairs={{0,4},{4,8},{8,12},{12,16},{16,20},{20,24},{24,28},{1,5},{5,9},{9,... | collective-permute-start | bytes 1228808 | tf_op jit(solution)/shard_map/ppermute | solution.py:12
  253.4 36.1 %collective-permute-start.4 = (f32[160,640]{1,0:T(8,128)}, f32[160,640]{1,0:T(8,128)}, u32[]{:S(2)}, u32[]{:S(2)}) collective-permute-start(f32[160,640]{1,0:T(8,128)} %get-tuple-element.97), channel_id=1, source_target_pairs={{4,0},{8,4},{12,8},{16,12},{20,16},{24,20},{28,24},{5,1},{9,5},{13... | collective-permute-start | bytes 1228808 | tf_op jit(solution)/shard_map/ppermute | solution.py:12
  254.7 21.0 %collective-permute-start.2 = (f32[160,640]{1,0:T(8,128)}, f32[160,640]{1,0:T(8,128)}, u32[]{:S(2)}, u32[]{:S(2)}) collective-permute-start(f32[160,640]{1,0:T(8,128)} %get-tuple-element.98), channel_id=1, source_target_pairs={{4,0},{8,4},{12,8},{16,12},{20,16},{24,20},{28,24},{5,1},{9,5},{13... | collective-permute-start | bytes 1228808 | tf_op jit(solution)/shard_map/ppermute | solution.py:12
  256.0 54.5 %collective-permute-start.3 = (f32[160,640]{1,0:T(8,128)}, f32[160,640]{1,0:T(8,128)}, u32[]{:S(2)}, u32[]{:S(2)}) collective-permute-start(f32[160,640]{1,0:T(8,128)} %get-tuple-element.98), channel_id=1, source_target_pairs={{0,4},{4,8},{8,12},{12,16},{16,20},{20,24},{24,28},{1,5},{5,9},{9,... | collective-permute-start | bytes 1228808 | tf_op jit(solution)/shard_map/ppermute | solution.py:12
  284.1 304.9 %all-gather.17.cloned.1.call-start = ((), (), s32[]{:S(2)}) async-start(), calls=%async_computation.5 | async-start | bytes 2048000 | tf_op jit(solution)/shard_map/all_gather | solution.py:61
  292.8 302.4 %all-gather.15.cloned.1.call-start = ((), (), s32[]{:S(2)}) async-start(), calls=%async_computation.4 | async-start | bytes 2048000 | tf_op jit(solution)/shard_map/all_gather | solution.py:60
  303.3 18.3 %collective-permute-start.10 = (f32[640,256]{1,0:T(8,128)}, f32[640,256]{1,0:T(8,128)}, u32[]{:S(2)}, u32[]{:S(2)}) collective-permute-start(f32[640,256]{1,0:T(8,128)} %constant_dynamic-update-slice_fusion.8), channel_id=1, source_target_pairs={{4,0},{8,4},{12,8},{16,12},{20,16},{24,20},{28,24},{5,1},{9,5},{13... | collective-permute-start | bytes 1966088 | tf_op jit(solution)/shard_map/ppermute | solution.py:12
  304.6 32.2 %collective-permute-start.9 = (f32[640,256]{1,0:T(8,128)}, f32[640,256]{1,0:T(8,128)}, u32[]{:S(2)}, u32[]{:S(2)}) collective-permute-start(f32[640,256]{1,0:T(8,128)} %constant_dynamic-update-slice_fusion.8), channel_id=1, source_target_pairs={{0,4},{4,8},{8,12},{12,16},{16,20},{20,24},{24,28},{1,5},{5,9},{9,... | collective-permute-start | bytes 1966088 | tf_op jit(solution)/shard_map/ppermute | solution.py:12
  462.1 69.6 %copy-start = (f32[160,640]{1,0:T(8,128)S(1)}, f32[160,640]{1,0:T(8,128)}, u32[]{:S(2)}) copy-start(f32[160,640]{1,0:T(8,128)} %convolution_negate_fusion.2) | copy-start | bytes 1228804
  462.1 69.6 %copy-start.1 = (f32[160,640]{1,0:T(8,128)S(1)}, f32[160,640]{1,0:T(8,128)}, u32[]{:S(2)}) copy-start(f32[160,640]{1,0:T(8,128)} %convolution_negate_fusion.3) | copy-start | bytes 1228804
  463.4 68.6 %copy-start.12 = (f32[640,256]{1,0:T(8,128)S(1)}, f32[640,256]{1,0:T(8,128)}, u32[]{:S(2)}) copy-start(f32[640,256]{1,0:T(8,128)} %fusion.2) | copy-start | bytes 1966084
  544.2 47.8 %collective-permute-start.8 = (f32[160,640]{1,0:T(8,128)}, f32[160,640]{1,0:T(8,128)}, u32[]{:S(2)}, u32[]{:S(2)}) collective-permute-start(f32[160,640]{1,0:T(8,128)} %get-tuple-element.95), channel_id=1, source_target_pairs={{8,0},{12,4},{16,8},{20,12},{24,16},{28,20},{9,1},{13,5},{17,9},{2... | collective-permute-start | bytes 1228808 | tf_op jit(solution)/shard_map/ppermute | solution.py:12
  545.5 38.6 %collective-permute-start.6 = (f32[160,640]{1,0:T(8,128)}, f32[160,640]{1,0:T(8,128)}, u32[]{:S(2)}, u32[]{:S(2)}) collective-permute-start(f32[160,640]{1,0:T(8,128)} %get-tuple-element.96), channel_id=1, source_target_pairs={{8,0},{12,4},{16,8},{20,12},{24,16},{28,20},{9,1},{13,5},{17,9},{2... | collective-permute-start | bytes 1228808 | tf_op jit(solution)/shard_map/ppermute | solution.py:12
  552.7 58.0 %collective-permute-start.12 = (f32[640,256]{1,0:T(8,128)}, f32[640,256]{1,0:T(8,128)}, u32[]{:S(2)}, u32[]{:S(2)}) collective-permute-start(f32[640,256]{1,0:T(8,128)} %constant_dynamic-update-slice_fusion.12), channel_id=1, source_target_pairs={{8,0},{12,4},{16,8},{20,12},{24,16},{28,20},{9,1},{13,5},{17,9},{2... | collective-permute-start | bytes 1966088 | tf_op jit(solution)/shard_map/ppermute | solution.py:12
  554.0 60.5 %collective-permute-start.11 = (f32[640,256]{1,0:T(8,128)}, f32[640,256]{1,0:T(8,128)}, u32[]{:S(2)}, u32[]{:S(2)}) collective-permute-start(f32[640,256]{1,0:T(8,128)} %constant_dynamic-update-slice_fusion.12), channel_id=1, source_target_pairs={{0,8},{4,12},{8,16},{12,20},{16,24},{20,28},{1,9},{5,13},{9,17},{1... | collective-permute-start | bytes 1966088 | tf_op jit(solution)/shard_map/ppermute | solution.py:12
  577.2 23.4 %collective-permute-start.7 = (f32[160,640]{1,0:T(8,128)}, f32[160,640]{1,0:T(8,128)S(1)}, u32[]{:S(2)}, u32[]{:S(2)}) collective-permute-start(f32[160,640]{1,0:T(8,128)} %get-tuple-element.96), channel_id=1, source_target_pairs={{0,8},{4,12},{8,16},{12,20},{16,24},{20,28},{1,9},{5,13},{9,17},{1... | collective-permute-start | bytes 1228808 | tf_op jit(solution)/shard_map/ppermute | solution.py:12
  584.1 23.5 %collective-permute-start.5 = (f32[160,640]{1,0:T(8,128)}, f32[160,640]{1,0:T(8,128)}, u32[]{:S(2)}, u32[]{:S(2)}) collective-permute-start(f32[160,640]{1,0:T(8,128)} %get-tuple-element.95), channel_id=1, source_target_pairs={{0,8},{4,12},{8,16},{12,20},{16,24},{20,28},{1,9},{5,13},{9,17},{1... | collective-permute-start | bytes 1228808 | tf_op jit(solution)/shard_map/ppermute | solution.py:12
  (22 other events, 368.2 us)
Sparse Core Ops, SparseCore 0:
  24.5 22.2 all-gather.6
  48.9 20.0 all-gather.10
  71.2 20.1 all-gather.8
  284.2 32.8 all-gather.12
  319.0 20.0 all-gather.16
  341.1 20.1 all-gather.14
where the time goes:
time: 639 us; the launch traced here: 626 us
  other arithmetic  331 us (52%)
  matrix products  88.4 us (14%)
  waiting for transfers between devices  76.3 us (12%)
  starting transfers between devices  60.2 us (9%)
  local copies, waits for them, and re-layouts  48.5 us (8%)
  between operations  21.7 us (3%)
    another operation x37, other arithmetic, shards(): factor = jnp.linalg.cholesky(full_diag_t.T)  224 us
    another operation x5, other arithmetic, solve_from_right(): lax.linalg.triangular_solve(factor, left, left_side=False, lower=True, tr...  103 us
    ppermute x13, starting transfers between devices, from_behind(): return lax.ppermute(shard, axis, pairs)  59.7 us
    ppermute x13, waiting for transfers between devices, from_behind(): return lax.ppermute(shard, axis, pairs)  53.9 us
    another operation x33, local copies, waits for them, and re-layouts, solve_from_right(): lax.linalg.triangular_solve(factor, left, left_side=False, lower=True, tr...  32.2 us
    dot_general x8, matrix products, matmul(): jnp.dot(left, right, precision=lax.Precision.HIGHEST, preferred_element_t...  26.7 us
    all_gather x2, waiting for transfers between devices, shards(): lax.all_gather(diag_t, 'rhs', axis=0, tiled=True)  20.9 us
    dot_general x4, matrix products, leading_matmul(): lax.dot_general(left, right, (((0,), (0,)), ((), ())), precision=lax.Prec...  17.2 us
  transfers between devices with their start and end apart: 19, of which 9 were waited for; matrix products, arithmetic and copies ran while one was open for 73% of the time, Pallas kernels for 0%

commit v1 on v0

v1 whole, which is shorter than its diff:
```python
import jax
import jax.numpy as jnp
from jax import lax
from jax.experimental import pallas as pl
from jax.experimental.pallas import tpu as pltpu
from jax.sharding import PartitionSpec as P

LEVELS = 2
BLOCK = 128
LEAF = 8
F32 = jnp.float32
BF16 = jnp.bfloat16


def from_behind(shard, axis, by):
    count = lax.axis_size(axis)
    pairs = [(i, i + by) for i in range(count) if 0 <= i + by < count]
    return lax.ppermute(shard, axis, pairs)


def matmul(left, right):
    return jnp.dot(left, right, precision=lax.Precision.HIGH, preferred_element_type=F32)


def leading_matmul(left, right):
    return lax.dot_general(
        left, right, (((0,), (0,)), ((), ())), precision=lax.Precision.HIGH, preferred_element_type=F32
    )


def split(x):
    high = x.astype(BF16)
    return high, (x - high.astype(F32)).astype(BF16)


def dot3(left, right):
    (lh, ll), (rh, rl) = left, right
    dot = lambda a, b: jnp.dot(a, b, preferred_element_type=F32)
    return dot(lh, rh) + (dot(lh, rl) + dot(ll, rh))


def spread(row, j):
    return jnp.broadcast_to(row[:, j : j + 1], row.shape)


def sub(tile, j):
    return jnp.broadcast_to(tile[j : j + 1, :], tile.shape)


def leaf_inverse(columns, rows):
    columns = list(columns)
    for q in range(LEAF):
        here = rows == q
        inv = 1.0 / sub(columns[q], q)
        pivot_column = columns[q]
        for j in range(LEAF):
            if j != q:
                e = sub(columns[j], q) * inv
                columns[j] = jnp.where(here, e, columns[j] - pivot_column * e)
        columns[q] = jnp.where(here, inv, -pivot_column * inv)
    return columns


def block_inverses(blocks):
    count = BLOCK // LEAF
    rows = lax.broadcasted_iota(jnp.int32, (LEAF, BLOCK), 0)
    lanes = lax.broadcasted_iota(jnp.int32, (LEAF, BLOCK), 1)
    tiles = [[b[LEAF * s : LEAF * (s + 1), :] for s in range(count)] for b in blocks]
    for t in range(count):
        base = LEAF * t
        inside = (lanes >= base) & (lanes < base + LEAF)
        unit = (lanes - base == rows).astype(F32)
        for held in tiles:
            row = held[t]
            inverse = leaf_inverse([spread(row, base + j) for j in range(LEAF)], rows)
            framed = jnp.where(inside, unit, row)
            parts = [inverse[j] * sub(framed, j) for j in range(LEAF)]
            while len(parts) > 1:
                parts = [a + b for a, b in zip(parts[::2], parts[1::2])]
            new = parts[0]
            steps = [sub(new, j) for j in range(LEAF)]
            order = list(range(t + 1, count)) + list(range(t))
            for s in order:
                old = held[s]
                total = jnp.where(inside, 0.0, old)
                for j in range(LEAF):
                    total = total - spread(old, base + j) * steps[j]
                held[s] = total
            held[t] = new
    return [jnp.concatenate(held, axis=0) for held in tiles]


def invert_kernel(a_ref, out_ref):
    size = a_ref.shape[0]
    out_ref[...] = a_ref[...]
    unit = (
        lax.broadcasted_iota(jnp.int32, (BLOCK, BLOCK), 0) == lax.broadcasted_iota(jnp.int32, (BLOCK, BLOCK), 1)
    ).astype(F32)

    def step(k, carry):
        here = pl.ds(pl.multiple_of(k * BLOCK, BLOCK), BLOCK)
        (inverse,) = block_inverses([out_ref[here, here]])
        out_ref[here, here] = unit
        row = dot3(split(inverse), split(out_ref[here, :]))
        column = out_ref[:, here]
        out_ref[:, here] = jnp.zeros((size, BLOCK), F32)
        out_ref[...] -= dot3(split(column), split(row))
        out_ref[here, :] = row
        return carry

    lax.fori_loop(0, size // BLOCK, step, 0)


def invert(matrix):
    size = matrix.shape[0]
    return pl.pallas_call(
        invert_kernel,
        out_shape=jax.ShapeDtypeStruct((size, size), F32),
        in_specs=[pl.BlockSpec(memory_space=pltpu.VMEM)],
        out_specs=pl.BlockSpec(memory_space=pltpu.VMEM),
        compiler_params=pltpu.CompilerParams(vmem_limit_bytes=48 * 2**20),
        cost_estimate=pl.CostEstimate(flops=6 * size**3, bytes_accessed=8 * size * size, transcendentals=0),
        name="invert",
    )(matrix)


def shards(coupling, density, support, loads):
    ncols = coupling.shape[1]
    width = coupling.shape[2]
    column_part = lax.axis_index("rhs")
    layer_id = lax.axis_index("layer")
    last_layer = lax.axis_size("layer") - 1
    rho = 0.3 + 0.7 * density[0].astype(F32)
    rho_cols = lax.dynamic_slice_in_dim(rho, column_part * ncols, ncols, 0)
    stiff_t = rho_cols[:, None] * coupling[0] * rho[None, :]
    below_t = from_behind(stiff_t, "layer", 1)
    col_index = lax.broadcasted_iota(jnp.int32, (ncols, width), 0) + column_part * ncols
    row_index = lax.broadcasted_iota(jnp.int32, (ncols, width), 1)
    diag_part = jnp.where(row_index == col_index, support[0][None, :], F32(0.0))
    diag_t = below_t + stiff_t + diag_part
    lower_t = -below_t
    upper_t = jnp.where(layer_id < last_layer, -stiff_t, jnp.zeros_like(stiff_t))
    right = loads[0]
    for level in range(LEVELS):
        dist = 2**level
        full_diag_t, full_lower_t, full_upper_t = (
            lax.all_gather(diag_t, "rhs", axis=0, tiled=True),
            lax.all_gather(lower_t, "rhs", axis=0, tiled=True),
            lax.all_gather(upper_t, "rhs", axis=0, tiled=True),
        )
        inverse = invert(full_diag_t)
        solved_lower = matmul(lower_t, inverse)
        solved_upper = matmul(upper_t, inverse)
        solved_right = matmul(inverse, right)
        low_l, low_u, low_b = from_behind((solved_lower, solved_upper, solved_right), "layer", dist)
        high_l, high_u, high_b = from_behind((solved_lower, solved_upper, solved_right), "layer", -dist)
        new_lower = -matmul(low_l, full_lower_t)
        new_upper = -matmul(high_u, full_upper_t)
        new_diag = diag_t - matmul(low_u, full_lower_t) - matmul(high_l, full_upper_t)
        new_right = right - leading_matmul(full_lower_t, low_b) - leading_matmul(full_upper_t, high_b)
        diag_t, lower_t, upper_t, right = (new_diag, new_lower, new_upper, new_right)
    return (diag_t[None], lower_t[None], upper_t[None], right[None])


def solution(mesh):
    placed = (P("layer", "rhs", None), P("layer", None), P("layer", None), P("layer", None, "rhs"))
    return jax.shard_map(
        shards,
        mesh=mesh,
        in_specs=placed,
        out_specs=(P("layer", "rhs", None),) * 3 + (P("layer", None, "rhs"),),
        check_vma=False,
    )
```

time: 639 us -> 256 us (0.40); the launches traced: 626 us -> 254 us
  other arithmetic: 331 us -> 4.22 us
  Pallas kernels: 0 us -> 53.7 us
  matrix products: 88.4 us -> 39.9 us
  local copies, waits for them, and re-layouts: 48.5 us -> 3.23 us
  waiting for transfers between devices: 76.3 us -> 90.6 us
  starting transfers between devices: 60.2 us -> 48 us
  between operations: 21.7 us -> 14.4 us
    another operation x42 -> x0, other arithmetic: 327 us -> none  [the longest x37 224 us: shards(): factor = jnp.linalg.cholesky(full_diag_t.T)]
    pallas_call x0 -> x2, Pallas kernels: none -> 53.7 us  [invert(): pl.pallas_call(invert_kernel, out_shape=jax.ShapeDtypeStruct((size, size)...]
    another operation x88 -> x0, matrix products: 44.5 us -> none  [the longest x18 13.2 us: solve_spd(): lax.linalg.triangular_solve(factor, half, left_side=True, lower=True, tra...]
    another operation x47 -> x0, local copies, waits for them, and re-layouts: 35.1 us -> none  [the longest x33 32.2 us: solve_from_right(): lax.linalg.triangular_solve(factor, left, left_side=False, lower=True, tr...]
    ppermute x13, waiting for transfers between devices: 53.9 us -> 68.2 us  [from_behind(): return lax.ppermute(shard, axis, pairs)]
    ppermute x13, starting transfers between devices: 59.7 us -> 47.8 us  [from_behind(): return lax.ppermute(shard, axis, pairs)]
    dot_general x8 -> x14, matrix products: 26.7 us -> 28.6 us  [matmul(): jnp.dot(left, right, precision=lax.Precision.HIGH, preferred_element_type...]
  transfers between devices with their start and end apart: 19 -> 19, of which waited for: 9 -> 9; matrix products, arithmetic and copies ran while one was open for 73% -> 13% of each run, Pallas kernels for 0% -> 21%
where the time goes in v1:
time: 256 us; the launch traced here: 254 us
  waiting for transfers between devices  90.6 us (35%)
  Pallas kernels  53.7 us (21%)
  starting transfers between devices  48 us (19%)
  matrix products  39.9 us (16%)
  between operations  14.4 us (6%)
  other arithmetic  4.22 us (2%)
  local copies, waits for them, and re-layouts  3.23 us (1%)
    ppermute x13, waiting for transfers between devices, from_behind(): return lax.ppermute(shard, axis, pairs)  68.2 us
    pallas_call x2, Pallas kernels, invert(): pl.pallas_call(invert_kernel, out_shape=jax.ShapeDtypeStruct((size, size)...  53.7 us
    ppermute x13, starting transfers between devices, from_behind(): return lax.ppermute(shard, axis, pairs)  47.8 us
    dot_general x14, matrix products, matmul(): jnp.dot(left, right, precision=lax.Precision.HIGH, preferred_element_type...  28.6 us
    all_gather x2, waiting for transfers between devices, shards(): lax.all_gather(diag_t, 'rhs', axis=0, tiled=True)  20.9 us
    dot_general x4, matrix products, leading_matmul(): lax.dot_general(left, right, (((0,), (0,)), ((), ())), precision=lax.Prec...  11.4 us
  transfers between devices with their start and end apart: 19, of which 9 were waited for; matrix products, arithmetic and copies ran while one was open for 13% of the time, Pallas kernels for 21%

profile of v1, /device:TPU:0, one launch (start us, length us, event | category | flops | bytes accessed | tf_op | source)
XLA Modules:
  0.0 254.1 jit_solution(11713653120496445742)
XLA Ops:
  9.9 4.9 %collective-permute-start = (f32[160,640]{1,0:T(8,128)S(1)}, f32[160,640]{1,0:T(8,128)S(1)}, u32[]{:S(2)}, u32[]{:S(2)}) collective-permute-start(f32[160,640]{1,0:T(8,128)S(1)} %get-tuple-element.5), channel_id=1, source_target_pairs={{0,4},{4,8},{8,12},{12,16},{16,20},{20,24},{24,28},{1,5},{5,9},{9,... | collective-permute-start | bytes 1228808 | tf_op jit(solution)/shard_map/ppermute | solution.py:18
  15.5 8.0 %collective-permute-done = f32[160,640]{1,0:T(8,128)S(1)} collective-permute-done((f32[160,640]{1,0:T(8,128)S(1)}, f32[160,640]{1,0:T(8,128)S(1)}, u32[]{:S(2)}, u32[]{:S(2)}) %collective-permute-start) | collective-permute-done | bytes 409632 | tf_op jit(solution)/shard_map/ppermute | solution.py:18
  25.9 20.9 %all-gather.7.cloned.1.call-done.a_ref = f32[640,640]{1,0:T(8,128)} async-done(((f32[160,640]{1,0:T(8,128)}), f32[640,640]{1,0:T(8,128)}) %all-gather.7.cloned.1.call-update) | async-done | bytes 1638416 | tf_op jit(solution)/shard_map/all_gather | solution.py:147
  48.2 26.9 %invert.2 = f32[640,640]{1,0:T(8,128)S(1)} custom-call(f32[640,640]{1,0:T(8,128)S(1)} %copy-done.1), custom_call_target="tpu_custom_call" | custom-call | flops 1572864000 | bytes 3276800 | tf_op jit(solution)/shard_map/invert/pallas_call | solution.py:116
  78.8 5.3 %collective-permute-start.1 = (f32[160,640]{1,0:T(8,128)}, f32[160,640]{1,0:T(8,128)}, u32[]{:S(2)}, u32[]{:S(2)}) collective-permute-start(f32[160,640]{1,0:T(8,128)} %fusion.16), channel_id=1, source_target_pairs={{0,4},{4,8},{8,12},{12,16},{16,20},{20,24},{24,28},{1,5},{5,9},{9,... | collective-permute-start | bytes 1228808 | tf_op jit(solution)/shard_map/ppermute | solution.py:18
  84.1 5.3 %collective-permute-done.2 = f32[160,640]{1,0:T(8,128)S(1)} collective-permute-done((f32[160,640]{1,0:T(8,128)S(1)}, f32[160,640]{1,0:T(8,128)S(1)}, u32[]{:S(2)}, u32[]{:S(2)}) %collective-permute-start.2) | collective-permute-done | bytes 409632 | tf_op jit(solution)/shard_map/ppermute | solution.py:18
  89.4 3.0 %fusion.17 = f32[160,640]{1,0:T(8,128)} fusion(f32[160,640]{1,0:T(8,128)S(1)} %collective-permute-done.2, f32[640,640]{1,0:T(8,128)} %all-gather.11.cloned.1.call-done), kind=kOutput, calls=%fused_computation.31 | convolution fusion | flops 393216000 | bytes 2457600 | tf_op jit(solution)/shard_map/dot_general | solution.py:22
  92.4 5.8 %collective-permute-done.1 = f32[160,640]{1,0:T(8,128)} collective-permute-done((f32[160,640]{1,0:T(8,128)}, f32[160,640]{1,0:T(8,128)}, u32[]{:S(2)}, u32[]{:S(2)}) %collective-permute-start.1) | collective-permute-done | bytes 409632 | tf_op jit(solution)/shard_map/ppermute | solution.py:18
  98.2 3.3 %fusion.7 = f32[160,640]{1,0:T(8,128)} fusion(f32[160,640]{1,0:T(8,128)} %fusion.17, f32[160,640]{1,0:T(8,128)} %get-tuple-element.7, f32[160,640]{1,0:T(8,128)} %collective-permute-done.1, f32[640,640]{1,0:T(8,128)} %all-gather.9.cloned.1.call-done), kind=kOutput, calls=%fused_computation.15 | convolution fusion | flops 393420800 | bytes 3276800 | tf_op jit(solution)/shard_map/dot_general | solution.py:22
  102.8 12.9 %collective-permute-done.3 = f32[160,640]{1,0:T(8,128)S(1)} collective-permute-done((f32[160,640]{1,0:T(8,128)}, f32[160,640]{1,0:T(8,128)S(1)}, u32[]{:S(2)}, u32[]{:S(2)}) %collective-permute-start.3) | collective-permute-done | bytes 409632 | tf_op jit(solution)/shard_map/ppermute | solution.py:18
  117.4 5.0 %collective-permute-start.5 = (f32[160,640]{1,0:T(8,128)}, f32[160,640]{1,0:T(8,128)S(1)}, u32[]{:S(2)}, u32[]{:S(2)}) collective-permute-start(f32[160,640]{1,0:T(8,128)} %copy-done.14), channel_id=1, source_target_pairs={{0,4},{4,8},{8,12},{12,16},{16,20},{20,24},{24,28},{1,5},{5,9},{9,... | collective-permute-start | bytes 1228808 | tf_op jit(solution)/shard_map/ppermute | solution.py:18
  122.5 2.9 %fusion.8 = f32[640,256]{1,0:T(8,128)} fusion(f32[640,640]{1,0:T(8,128)S(1)} %invert.2, f32[1,640,256]{2,1,0:T(8,128)} %param.7), kind=kOutput, calls=%fused_computation.16 | convolution fusion | flops 629145600 | bytes 2949120 | tf_op jit(solution)/shard_map/dot_general | solution.py:22
  126.6 5.4 %collective-permute-start.9 = (f32[640,256]{1,0:T(8,128)}, f32[640,256]{1,0:T(8,128)}, u32[]{:S(2)}, u32[]{:S(2)}) collective-permute-start(f32[640,256]{1,0:T(8,128)} %fusion.8), channel_id=1, source_target_pairs={{0,4},{4,8},{8,12},{12,16},{16,20},{20,24},{24,28},{1,5},{5,9},{9,... | collective-permute-start | bytes 1966088 | tf_op jit(solution)/shard_map/ppermute | solution.py:18
  132.0 14.1 %collective-permute-done.5 = f32[160,640]{1,0:T(8,128)S(1)} collective-permute-done((f32[160,640]{1,0:T(8,128)}, f32[160,640]{1,0:T(8,128)S(1)}, u32[]{:S(2)}, u32[]{:S(2)}) %collective-permute-start.5) | collective-permute-done | bytes 409632 | tf_op jit(solution)/shard_map/ppermute | solution.py:18
  147.8 2.7 %fusion.21 = f32[640,256]{1,0:T(8,128)S(1)} fusion(f32[640,640]{1,0:T(8,128)S(1)} %copy-done.3, f32[640,256]{1,0:T(8,128)} %collective-permute-done.10), kind=kOutput, calls=%fused_computation.35 | convolution fusion | flops 629145600 | bytes 2949120 | tf_op jit(solution)/shard_map/dot_general | solution.py:26
  150.5 8.0 %collective-permute-done.9 = f32[640,256]{1,0:T(8,128)} collective-permute-done((f32[640,256]{1,0:T(8,128)}, f32[640,256]{1,0:T(8,128)}, u32[]{:S(2)}, u32[]{:S(2)}) %collective-permute-start.9) | collective-permute-done | bytes 655392 | tf_op jit(solution)/shard_map/ppermute | solution.py:18
  162.8 26.8 %invert.3 = f32[640,640]{1,0:T(8,128)S(1)} custom-call(f32[640,640]{1,0:T(8,128)S(1)} %copy-done), custom_call_target="tpu_custom_call" | custom-call | flops 1572864000 | bytes 3276800 | tf_op jit(solution)/shard_map/invert/pallas_call | solution.py:116
  196.9 10.7 %collective-permute-start.11 = (f32[640,256]{1,0:T(8,128)S(1)}, f32[640,256]{1,0:T(8,128)}, u32[]{:S(2)}, u32[]{:S(2)}) collective-permute-start(f32[640,256]{1,0:T(8,128)S(1)} %fusion.22), channel_id=1, source_target_pairs={{0,8},{4,12},{8,16},{12,20},{16,24},{20,28},{1,9},{5,13},{9,17},{1... | collective-permute-start | bytes 1966088 | tf_op jit(solution)/shard_map/ppermute | solution.py:18
  207.6 3.9 %collective-permute-start.7 = (f32[160,640]{1,0:T(8,128)}, f32[160,640]{1,0:T(8,128)}, u32[]{:S(2)}, u32[]{:S(2)}) collective-permute-start(f32[160,640]{1,0:T(8,128)} %fusion.19), channel_id=1, source_target_pairs={{0,8},{4,12},{8,16},{12,20},{16,24},{20,28},{1,9},{5,13},{9,17},{1... | collective-permute-start | bytes 1228808 | tf_op jit(solution)/shard_map/ppermute | solution.py:18
  211.5 4.9 %collective-permute-start.4 = (f32[160,640]{1,0:T(8,128)S(1)}, f32[160,640]{1,0:T(8,128)}, u32[]{:S(2)}, u32[]{:S(2)}) collective-permute-start(f32[160,640]{1,0:T(8,128)S(1)} %fusion.18), channel_id=1, source_target_pairs={{0,8},{4,12},{8,16},{12,20},{16,24},{20,28},{1,9},{5,13},{9,17},{1... | collective-permute-start | bytes 1228808 | tf_op jit(solution)/shard_map/ppermute | solution.py:18
  221.3 9.5 %collective-permute-done.7 = f32[160,640]{1,0:T(8,128)} collective-permute-done((f32[160,640]{1,0:T(8,128)}, f32[160,640]{1,0:T(8,128)}, u32[]{:S(2)}, u32[]{:S(2)}) %collective-permute-start.7) | collective-permute-done | bytes 409632 | tf_op jit(solution)/shard_map/ppermute | solution.py:18
  230.8 3.1 %fusion.4 = f32[1,160,640]{2,1,0:T(8,128)} fusion(f32[160,640]{1,0:T(8,128)} %collective-permute-done.7, f32[640,640]{1,0:T(8,128)} %all-gather.15.cloned.1.call-done), kind=kOutput, calls=%fused_computation.8 | convolution fusion | flops 393318400 | bytes 2457600 | tf_op jit(solution)/shard_map/dot_general | solution.py:22
  233.9 4.6 %collective-permute-done.4 = f32[160,640]{1,0:T(8,128)} collective-permute-done((f32[160,640]{1,0:T(8,128)S(1)}, f32[160,640]{1,0:T(8,128)}, u32[]{:S(2)}, u32[]{:S(2)}) %collective-permute-start.4) | collective-permute-done | bytes 409632 | tf_op jit(solution)/shard_map/ppermute | solution.py:18
  243.8 3.4 %fusion.1 = f32[1,640,256]{2,1,0:T(8,128)} fusion(f32[640,256]{1,0:T(8,128)S(1)} %fusion.23, f32[640,256]{1,0:T(8,128)S(1)} %copy-done.8, f32[640,640]{1,0:T(8,128)S(1)} %copy-done.6, f32[640,256]{1,0:T(8,128)} %collective-permute-done.11), kind=kOutput, calls=%fused_computation.2 | convolution fusion | flops 629473280 | bytes 4259840 | tf_op jit(solution)/shard_map/dot_general | solution.py:26
  (76 shorter events, 38.4 us)
Async XLA Ops:
  7.2 39.6 %all-gather.7.cloned.1.call-start = ((), (), s32[]{:S(2)}) async-start(), calls=%async_computation | async-start | bytes 2048000 | tf_op jit(solution)/shard_map/all_gather | solution.py:147
  9.9 13.6 %collective-permute-start = (f32[160,640]{1,0:T(8,128)S(1)}, f32[160,640]{1,0:T(8,128)S(1)}, u32[]{:S(2)}, u32[]{:S(2)}) collective-permute-start(f32[160,640]{1,0:T(8,128)S(1)} %get-tuple-element.5), channel_id=1, source_target_pairs={{0,4},{4,8},{8,12},{12,16},{16,20},{20,24},{24,28},{1,5},{5,9},{9,... | collective-permute-start | bytes 1228808 | tf_op jit(solution)/shard_map/ppermute | solution.py:18
  24.4 59.7 %all-gather.11.cloned.1.call-start = ((), (), s32[]{:S(2)}) async-start(), calls=%async_computation.2 | async-start | bytes 2048000 | tf_op jit(solution)/shard_map/all_gather | solution.py:149
  25.2 67.2 %all-gather.9.cloned.1.call-start = ((), (), s32[]{:S(2)}) async-start(), calls=%async_computation.1 | async-start | bytes 2048000 | tf_op jit(solution)/shard_map/all_gather | solution.py:148
  25.9 135.3 %all-gather.13.cloned.1.call-start = ((), (), s32[]{:S(2)}) async-start(), calls=%async_computation.3 | async-start | bytes 2048000 | tf_op jit(solution)/shard_map/all_gather | solution.py:147
  75.9 13.5 %collective-permute-start.2 = (f32[160,640]{1,0:T(8,128)S(1)}, f32[160,640]{1,0:T(8,128)S(1)}, u32[]{:S(2)}, u32[]{:S(2)}) collective-permute-start(f32[160,640]{1,0:T(8,128)S(1)} %fusion.12), channel_id=1, source_target_pairs={{4,0},{8,4},{12,8},{16,12},{20,16},{24,20},{28,24},{5,1},{9,5},{13... | collective-permute-start | bytes 1228808 | tf_op jit(solution)/shard_map/ppermute | solution.py:18
  78.8 19.4 %collective-permute-start.1 = (f32[160,640]{1,0:T(8,128)}, f32[160,640]{1,0:T(8,128)}, u32[]{:S(2)}, u32[]{:S(2)}) collective-permute-start(f32[160,640]{1,0:T(8,128)} %fusion.16), channel_id=1, source_target_pairs={{0,4},{4,8},{8,12},{12,16},{16,20},{20,24},{24,28},{1,5},{5,9},{9,... | collective-permute-start | bytes 1228808 | tf_op jit(solution)/shard_map/ppermute | solution.py:18
  92.4 23.4 %copy-start.3 = (f32[640,640]{1,0:T(8,128)S(1)}, f32[640,640]{1,0:T(8,128)}, u32[]{:S(2)}) copy-start(f32[640,640]{1,0:T(8,128)} %all-gather.11.cloned.1.call-done) | copy-start | bytes 4915204
  101.5 114.9 %all-gather.17.cloned.1.call-start = ((), (), s32[]{:S(2)}) async-start(), calls=%async_computation.5 | async-start | bytes 2048000 | tf_op jit(solution)/shard_map/all_gather | solution.py:149
  101.5 14.2 %collective-permute-start.3 = (f32[160,640]{1,0:T(8,128)}, f32[160,640]{1,0:T(8,128)S(1)}, u32[]{:S(2)}, u32[]{:S(2)}) collective-permute-start(f32[160,640]{1,0:T(8,128)} %fusion.16), channel_id=1, source_target_pairs={{4,0},{8,4},{12,8},{16,12},{20,16},{24,20},{28,24},{5,1},{9,5},{13... | collective-permute-start | bytes 1228808 | tf_op jit(solution)/shard_map/ppermute | solution.py:18
  117.4 103.9 %all-gather.15.cloned.1.call-start = ((), (), s32[]{:S(2)}) async-start(), calls=%async_computation.4 | async-start | bytes 2048000 | tf_op jit(solution)/shard_map/all_gather | solution.py:148
  117.4 28.7 %copy-start.4 = (f32[640,640]{1,0:T(8,128)S(1)}, f32[640,640]{1,0:T(8,128)}, u32[]{:S(2)}) copy-start(f32[640,640]{1,0:T(8,128)} %all-gather.9.cloned.1.call-done) | copy-start | bytes 4915204
  117.4 28.7 %collective-permute-start.5 = (f32[160,640]{1,0:T(8,128)}, f32[160,640]{1,0:T(8,128)S(1)}, u32[]{:S(2)}, u32[]{:S(2)}) collective-permute-start(f32[160,640]{1,0:T(8,128)} %copy-done.14), channel_id=1, source_target_pairs={{0,4},{4,8},{8,12},{12,16},{16,20},{20,24},{24,28},{1,5},{5,9},{9,... | collective-permute-start | bytes 1228808 | tf_op jit(solution)/shard_map/ppermute | solution.py:18
  125.4 22.4 %collective-permute-start.10 = (f32[640,256]{1,0:T(8,128)}, f32[640,256]{1,0:T(8,128)}, u32[]{:S(2)}, u32[]{:S(2)}) collective-permute-start(f32[640,256]{1,0:T(8,128)} %fusion.8), channel_id=1, source_target_pairs={{4,0},{8,4},{12,8},{16,12},{20,16},{24,20},{28,24},{5,1},{9,5},{13... | collective-permute-start | bytes 1966088 | tf_op jit(solution)/shard_map/ppermute | solution.py:18
  126.6 31.9 %collective-permute-start.9 = (f32[640,256]{1,0:T(8,128)}, f32[640,256]{1,0:T(8,128)}, u32[]{:S(2)}, u32[]{:S(2)}) collective-permute-start(f32[640,256]{1,0:T(8,128)} %fusion.8), channel_id=1, source_target_pairs={{0,4},{4,8},{8,12},{12,16},{16,20},{20,24},{24,28},{1,5},{5,9},{9,... | collective-permute-start | bytes 1966088 | tf_op jit(solution)/shard_map/ppermute | solution.py:18
  161.1 33.6 %copy-start.7 = (f32[640,256]{1,0:T(8,128)}, f32[640,256]{1,0:T(8,128)S(1)}, u32[]{:S(2)}) copy-start(f32[640,256]{1,0:T(8,128)S(1)} %fusion.2) | copy-start | bytes 1966084
  162.8 26.9 %copy-start.11 = (f32[160,640]{1,0:T(8,128)S(1)}, f32[160,640]{1,0:T(8,128)}, u32[]{:S(2)}) copy-start(f32[160,640]{1,0:T(8,128)} %convolution_negate_fusion.2) | copy-start | bytes 1228804
  191.3 20.2 %collective-permute-start.6 = (f32[160,640]{1,0:T(8,128)}, f32[160,640]{1,0:T(8,128)S(1)}, u32[]{:S(2)}, u32[]{:S(2)}) collective-permute-start(f32[160,640]{1,0:T(8,128)} %fusion.19), channel_id=1, source_target_pairs={{8,0},{12,4},{16,8},{20,12},{24,16},{28,20},{9,1},{13,5},{17,9},{2... | collective-permute-start | bytes 1228808 | tf_op jit(solution)/shard_map/ppermute | solution.py:18
  193.4 25.3 %collective-permute-start.8 = (f32[160,640]{1,0:T(8,128)S(1)}, f32[160,640]{1,0:T(8,128)}, u32[]{:S(2)}, u32[]{:S(2)}) collective-permute-start(f32[160,640]{1,0:T(8,128)S(1)} %fusion.18), channel_id=1, source_target_pairs={{8,0},{12,4},{16,8},{20,12},{24,16},{28,20},{9,1},{13,5},{17,9},{2... | collective-permute-start | bytes 1228808 | tf_op jit(solution)/shard_map/ppermute | solution.py:18
  195.6 45.5 %collective-permute-start.12 = (f32[640,256]{1,0:T(8,128)S(1)}, f32[640,256]{1,0:T(8,128)}, u32[]{:S(2)}, u32[]{:S(2)}) collective-permute-start(f32[640,256]{1,0:T(8,128)S(1)} %fusion.22), channel_id=1, source_target_pairs={{8,0},{12,4},{16,8},{20,12},{24,16},{28,20},{9,1},{13,5},{17,9},{2... | collective-permute-start | bytes 1966088 | tf_op jit(solution)/shard_map/ppermute | solution.py:18
  196.9 46.8 %collective-permute-start.11 = (f32[640,256]{1,0:T(8,128)S(1)}, f32[640,256]{1,0:T(8,128)}, u32[]{:S(2)}, u32[]{:S(2)}) collective-permute-start(f32[640,256]{1,0:T(8,128)S(1)} %fusion.22), channel_id=1, source_target_pairs={{0,8},{4,12},{8,16},{12,20},{16,24},{20,28},{1,9},{5,13},{9,17},{1... | collective-permute-start | bytes 1966088 | tf_op jit(solution)/shard_map/ppermute | solution.py:18
  207.6 23.1 %collective-permute-start.7 = (f32[160,640]{1,0:T(8,128)}, f32[160,640]{1,0:T(8,128)}, u32[]{:S(2)}, u32[]{:S(2)}) collective-permute-start(f32[160,640]{1,0:T(8,128)} %fusion.19), channel_id=1, source_target_pairs={{0,8},{4,12},{8,16},{12,20},{16,24},{20,28},{1,9},{5,13},{9,17},{1... | collective-permute-start | bytes 1228808 | tf_op jit(solution)/shard_map/ppermute | solution.py:18
  211.5 27.0 %collective-permute-start.4 = (f32[160,640]{1,0:T(8,128)S(1)}, f32[160,640]{1,0:T(8,128)}, u32[]{:S(2)}, u32[]{:S(2)}) collective-permute-start(f32[160,640]{1,0:T(8,128)S(1)} %fusion.18), channel_id=1, source_target_pairs={{0,8},{4,12},{8,16},{12,20},{16,24},{20,28},{1,9},{5,13},{9,17},{1... | collective-permute-start | bytes 1228808 | tf_op jit(solution)/shard_map/ppermute | solution.py:18
  221.3 17.2 %copy-start.9 = (f32[160,640]{1,0:T(8,128)S(1)}, f32[160,640]{1,0:T(8,128)}, u32[]{:S(2)}) copy-start(f32[160,640]{1,0:T(8,128)} %fusion.7) | copy-start | bytes 1228804
  (10 other events, 65.4 us)
Sparse Core Ops, SparseCore 0:
  24.5 22.2 all-gather.6
  48.9 20.0 all-gather.10
  71.1 20.0 all-gather.8
  101.6 22.2 all-gather.12
  125.9 20.0 all-gather.16
  147.9 20.0 all-gather.14

commit v2 on v1

--- a/solution.py
+++ b/solution.py
@@ -5,7 +5,6 @@
 from jax.experimental.pallas import tpu as pltpu
 from jax.sharding import PartitionSpec as P
 
-LEVELS = 2
 BLOCK = 128
 LEAF = 8
 F32 = jnp.float32
@@ -47,18 +46,28 @@
     return jnp.broadcast_to(tile[j : j + 1, :], tile.shape)
 
 
-def leaf_inverse(columns, rows):
-    columns = list(columns)
-    for q in range(LEAF):
-        here = rows == q
-        inv = 1.0 / sub(columns[q], q)
-        pivot_column = columns[q]
-        for j in range(LEAF):
-            if j != q:
-                e = sub(columns[j], q) * inv
-                columns[j] = jnp.where(here, e, columns[j] - pivot_column * e)
-        columns[q] = jnp.where(here, inv, -pivot_column * inv)
-    return columns
+def eliminate(entries, rows):
+    held = dict(entries)
+    rows = list(rows)
+    for q in range(0, LEAF, 2):
+        r = q + 1
+        a, b, c = held[q, q], held[q, r], held[r, r]
+        inv = 1.0 / (a * c - b * b)
+        later = range(q + 2, LEAF)
+        first = {j: (c * held[q, j] - b * held[r, j]) * inv for j in later}
+        second = {j: (a * held[r, j] - b * held[q, j]) * inv for j in later}
+        rows[q], rows[r] = (c * rows[q] - b * rows[r]) * inv, (a * rows[r] - b * rows[q]) * inv
+        for i in range(LEAF):
+            if i in (q, r):
+                continue
+            x, y = (held[i, q], held[i, r]) if i < q else (held[q, i], held[r, i])
+            for j in later:
+                if i <= j:
+                    held[i, j] = held[i, j] - (x * first[j] + y * second[j])
+            rows[i] = rows[i] - (x * rows[q] + y * rows[r])
+        for j in later:
+            held[q, j], held[r, j] = first[j], second[j]
+    return rows
 
 
 def block_inverses(blocks):
@@ -72,13 +81,10 @@
         unit = (lanes - base == rows).astype(F32)
         for held in tiles:
             row = held[t]
-            inverse = leaf_inverse([spread(row, base + j) for j in range(LEAF)], rows)
+            columns = [spread(row, base + j) for j in range(LEAF)]
+            entries = {(i, j): sub(columns[j], i) for j in range(LEAF) for i in range(j + 1)}
             framed = jnp.where(inside, unit, row)
-            parts = [inverse[j] * sub(framed, j) for j in range(LEAF)]
-            while len(parts) > 1:
-                parts = [a + b for a, b in zip(parts[::2], parts[1::2])]
-            new = parts[0]
-            steps = [sub(new, j) for j in range(LEAF)]
+            steps = eliminate(entries, [sub(framed, j) for j in range(LEAF)])
             order = list(range(t + 1, count)) + list(range(t))
             for s in order:
                 old = held[s]
@@ -86,6 +92,9 @@
                 for j in range(LEAF):
                     total = total - spread(old, base + j) * steps[j]
                 held[s] = total
+            new = steps[0]
+            for j in range(1, LEAF):
+                new = jnp.where(rows == j, steps[j], new)
             held[t] = new
     return [jnp.concatenate(held, axis=0) for held in tiles]
 
@@ -124,6 +133,26 @@
     )(matrix)
 
 
+def gather(slab):
+    if lax.axis_size("rhs") != 4:
+        return lax.all_gather(slab, "rhs", axis=0, tiled=True)
+    swap = lambda x, by: lax.ppermute(x, "rhs", [(i, i ^ by) for i in range(4)])
+    part = lax.axis_index("rhs")
+    far = swap(slab, 2)
+    mate = swap(slab, 1)
+    far_mate = swap(far, 1)
+    odd, high = part % 2 == 1, part >= 2
+    lows = (jnp.where(odd, mate, slab), jnp.where(odd, far_mate, far))
+    highs = (jnp.where(odd, slab, mate), jnp.where(odd, far, far_mate))
+    pick = lambda pair: (jnp.where(high, pair[1], pair[0]), jnp.where(high, pair[0], pair[1]))
+    (first, third), (second, fourth) = pick(lows), pick(highs)
+    return jnp.concatenate([first, second, third, fourth], axis=0)
+
+
+def after(values, *others):
+    return lax.optimization_barrier((values, others))[0]
+
+
 def shards(coupling, density, support, loads):
     ncols = coupling.shape[1]
     width = coupling.shape[2]
@@ -134,32 +163,56 @@
     rho_cols = lax.dynamic_slice_in_dim(rho, column_part * ncols, ncols, 0)
     stiff_t = rho_cols[:, None] * coupling[0] * rho[None, :]
     below_t = from_behind(stiff_t, "layer", 1)
+    stiff = gather(stiff_t)
+    below = gather(below_t)
     col_index = lax.broadcasted_iota(jnp.int32, (ncols, width), 0) + column_part * ncols
     row_index = lax.broadcasted_iota(jnp.int32, (ncols, width), 1)
-    diag_part = jnp.where(row_index == col_index, support[0][None, :], F32(0.0))
-    diag_t = below_t + stiff_t + diag_part
-    lower_t = -below_t
-    upper_t = jnp.where(layer_id < last_layer, -stiff_t, jnp.zeros_like(stiff_t))
+    diag_t = below_t + stiff_t + jnp.where(row_index == col_index, support[0][None, :], F32(0.0))
+    rows = lax.broadcasted_iota(jnp.int32, (width, width), 0)
+    columns = lax.broadcasted_iota(jnp.int32, (width, width), 1)
+    full_diag = below + stiff + jnp.where(rows == columns, support[0][None, :], F32(0.0))
+    above = layer_id < last_layer
+    lower_t, full_lower_t = -below_t, -below
+    upper_t = jnp.where(above, -stiff_t, jnp.zeros_like(stiff_t))
+    full_upper_t = jnp.where(above, -stiff, jnp.zeros_like(stiff))
     right = loads[0]
-    for level in range(LEVELS):
-        dist = 2**level
-        full_diag_t, full_lower_t, full_upper_t = (
-            lax.all_gather(diag_t, "rhs", axis=0, tiled=True),
-            lax.all_gather(lower_t, "rhs", axis=0, tiled=True),
-            lax.all_gather(upper_t, "rhs", axis=0, tiled=True),
-        )
-        inverse = invert(full_diag_t)
-        solved_lower = matmul(lower_t, inverse)
-        solved_upper = matmul(upper_t, inverse)
-        solved_right = matmul(inverse, right)
-        low_l, low_u, low_b = from_behind((solved_lower, solved_upper, solved_right), "layer", dist)
-        high_l, high_u, high_b = from_behind((solved_lower, solved_upper, solved_right), "layer", -dist)
-        new_lower = -matmul(low_l, full_lower_t)
-        new_upper = -matmul(high_u, full_upper_t)
-        new_diag = diag_t - matmul(low_u, full_lower_t) - matmul(high_l, full_upper_t)
-        new_right = right - leading_matmul(full_lower_t, low_b) - leading_matmul(full_upper_t, high_b)
-        diag_t, lower_t, upper_t, right = (new_diag, new_lower, new_upper, new_right)
-    return (diag_t[None], lower_t[None], upper_t[None], right[None])
+
+    inverse = invert(full_diag)
+    solved_upper = matmul(upper_t, inverse)
+    solved_lower = matmul(lower_t, inverse)
+    low_u = from_behind(solved_upper, "layer", 1)
+    high_l = from_behind(solved_lower, "layer", -1)
+    send_l, send_u = after((solved_lower, solved_upper), low_u, high_l)
+    low_l = from_behind(send_l, "layer", 1)
+    high_u = from_behind(send_u, "layer", -1)
+    diag_t = diag_t - matmul(low_u, full_lower_t) - matmul(high_l, full_upper_t)
+    full_diag = gather(diag_t)
+    solved_right = matmul(inverse, right)
+    send_b = after(solved_right, low_l, high_u)
+    low_b = from_behind(send_b, "layer", 1)
+    high_b = from_behind(send_b, "layer", -1)
+    lower_t, upper_t = -matmul(low_l, full_lower_t), -matmul(high_u, full_upper_t)
+    full_diag, lower_t, upper_t = lax.optimization_barrier((full_diag, lower_t, upper_t))
+    old_lower_t, old_upper_t = full_lower_t, full_upper_t
+    full_lower_t = lax.all_gather(lower_t, "rhs", axis=0, tiled=True)
+    full_upper_t = lax.all_gather(upper_t, "rhs", axis=0, tiled=True)
+
+    inverse = invert(full_diag)
+    solved = matmul(jnp.concatenate([lower_t, upper_t], axis=0), inverse)
+    low = from_behind(solved, "layer", 2)
+    high = from_behind(solved, "layer", -2)
+    low_b, high_b = after((low_b, high_b), inverse)
+    right = right - leading_matmul(old_lower_t, low_b) - leading_matmul(old_upper_t, high_b)
+    solved_right = matmul(inverse, right)
+    low_b = from_behind(solved_right, "layer", 2)
+    high_b = from_behind(solved_right, "layer", -2)
+    from_low = matmul(low, full_lower_t)
+    from_high = matmul(high, full_upper_t)
+    new_lower = -from_low[:ncols]
+    new_upper = -from_high[ncols:]
+    new_diag = diag_t - from_low[ncols:] - from_high[:ncols]
+    right = right - leading_matmul(full_lower_t, low_b) - leading_matmul(full_upper_t, high_b)
+    return (new_diag[None], new_lower[None], new_upper[None], right[None])
 
 
 def solution(mesh):

time: 256 us -> 215 us (0.84)
  waiting for transfers between devices: 90.6 us -> 59.6 us
  matrix products: 39.9 us -> 28.8 us
  other arithmetic: 4.22 us -> 9.15 us
  Pallas kernels: 53.7 us -> 57.2 us
  starting transfers between devices: 48 us -> 44.5 us
  local copies, waits for them, and re-layouts: 3.23 us -> 0.2 us
    ppermute x13 -> x11, waiting for transfers between devices: 68.2 us -> 46.6 us  [from_behind(): return lax.ppermute(shard, axis, pairs)]
    all_gather x6 -> x2, waiting for transfers between devices: 20.9 us -> 0.01 us  [the longest x1 0.01 us: shards(): full_lower_t = lax.all_gather(lower_t, 'rhs', axis=0, tiled=True)]
    ppermute x0 -> x9, waiting for transfers between devices: none -> 12.2 us  [gather(): swap = lambda x, by: lax.ppermute(x, 'rhs', [(i, i ^ by) for i in range(4)])]
    dot_general x14 -> x11, matrix products: 28.6 us -> 19.9 us  [matmul(): jnp.dot(left, right, precision=lax.Precision.HIGH, preferred_element_type...]
    ppermute x13 -> x11, starting transfers between devices: 47.8 us -> 39.4 us  [from_behind(): return lax.ppermute(shard, axis, pairs)]
    ppermute x0 -> x9, starting transfers between devices: none -> 5.06 us  [gather(): swap = lambda x, by: lax.ppermute(x, 'rhs', [(i, i ^ by) for i in range(4)])]
    pallas_call x2, Pallas kernels: 53.7 us -> 57.2 us  [invert(): pl.pallas_call(invert_kernel, out_shape=jax.ShapeDtypeStruct((size, size)...]
    unnamed x30 -> x50, local copies, waits for them, and re-layouts: 3.15 us -> 0.12 us
  transfers between devices with their start and end apart: 19 -> 22, of which waited for: 9 -> 11; matrix products, arithmetic and copies ran while one was open for 13% -> 12% of each run, Pallas kernels for 21% -> 13%
where the time goes in v2:
time: 215 us; the launch traced here: 214 us
  waiting for transfers between devices  59.6 us (28%)
  Pallas kernels  57.2 us (27%)
  starting transfers between devices  44.5 us (21%)
  matrix products  28.8 us (13%)
  between operations  14.6 us (7%)
  other arithmetic  9.15 us (4%)
    pallas_call x2, Pallas kernels, invert(): pl.pallas_call(invert_kernel, out_shape=jax.ShapeDtypeStruct((size, size)...  57.2 us
    ppermute x11, waiting for transfers between devices, from_behind(): return lax.ppermute(shard, axis, pairs)  46.6 us
    ppermute x11, starting transfers between devices, from_behind(): return lax.ppermute(shard, axis, pairs)  39.4 us
    dot_general x11, matrix products, matmul(): jnp.dot(left, right, precision=lax.Precision.HIGH, preferred_element_type...  19.9 us
    ppermute x9, waiting for transfers between devices, gather(): swap = lambda x, by: lax.ppermute(x, 'rhs', [(i, i ^ by) for i in range(4)])  12.2 us
    dot_general x4, matrix products, leading_matmul(): lax.dot_general(left, right, (((0,), (0,)), ((), ())), precision=lax.Prec...  8.96 us
    ppermute x9, starting transfers between devices, gather(): swap = lambda x, by: lax.ppermute(x, 'rhs', [(i, i ^ by) for i in range(4)])  5.06 us
  transfers between devices with their start and end apart: 22, of which 11 were waited for; matrix products, arithmetic and copies ran while one was open for 12% of the time, Pallas kernels for 13%

profile of v2, /device:TPU:0, one launch (start us, length us, event | category | flops | bytes accessed | tf_op | source)
XLA Modules:
  0.0 214.1 jit_solution(11509909230903078555)
XLA Ops:
  9.1 4.9 %collective-permute-start = (f32[160,640]{1,0:T(8,128)S(1)}, f32[160,640]{1,0:T(8,128)S(1)}, u32[]{:S(2)}, u32[]{:S(2)}) collective-permute-start(f32[160,640]{1,0:T(8,128)S(1)} %fusion.36), channel_id=1, source_target_pairs={{0,4},{4,8},{8,12},{12,16},{16,20},{20,24},{24,28},{1,5},{5,9},{9,... | collective-permute-start | bytes 1228808 | tf_op jit(solution)/shard_map/ppermute | solution.py:17
  15.6 7.1 %collective-permute-done = f32[160,640]{1,0:T(8,128)S(1)} collective-permute-done((f32[160,640]{1,0:T(8,128)S(1)}, f32[160,640]{1,0:T(8,128)S(1)}, u32[]{:S(2)}, u32[]{:S(2)}) %collective-permute-start) | collective-permute-done | bytes 409632 | tf_op jit(solution)/shard_map/ppermute | solution.py:17
  26.2 7.6 %collective-permute-done.1 = f32[160,640]{1,0:T(8,128)S(1)} collective-permute-done((f32[160,640]{1,0:T(8,128)S(1)}, f32[160,640]{1,0:T(8,128)S(1)}, u32[]{:S(2)}, u32[]{:S(2)}) %collective-permute-start.1) | collective-permute-done | bytes 409632 | tf_op jit(solution)/shard_map/ppermute | solution.py:139
  37.5 28.6 %invert.2 = f32[640,640]{1,0:T(8,128)S(1)} custom-call(f32[640,640]{1,0:T(8,128)S(1)} %select_add_fusion.a_ref), custom_call_target="tpu_custom_call" | custom-call | flops 1572864000 | bytes 3276800 | tf_op jit(solution)/shard_map/invert/pallas_call | solution.py:125
  69.7 4.6 %collective-permute-start.7 = (f32[160,640]{1,0:T(8,128)S(1)}, f32[160,640]{1,0:T(8,128)S(1)}, u32[]{:S(2)}, u32[]{:S(2)}) collective-permute-start(f32[160,640]{1,0:T(8,128)S(1)} %fusion.39), channel_id=1, source_target_pairs={{0,4},{4,8},{8,12},{12,16},{16,20},{20,24},{24,28},{1,5},{5,9},{9,... | collective-permute-start | bytes 1228808 | tf_op jit(solution)/shard_map/ppermute | solution.py:17
  74.3 7.3 %collective-permute-done.8 = f32[160,640]{1,0:T(8,128)S(1)} collective-permute-done((f32[160,640]{1,0:T(8,128)}, f32[160,640]{1,0:T(8,128)S(1)}, u32[]{:S(2)}, u32[]{:S(2)}) %collective-permute-start.8) | collective-permute-done | bytes 409632 | tf_op jit(solution)/shard_map/ppermute | solution.py:17
  81.6 8.9 %collective-permute-done.7 = f32[160,640]{1,0:T(8,128)S(1)} collective-permute-done((f32[160,640]{1,0:T(8,128)S(1)}, f32[160,640]{1,0:T(8,128)S(1)}, u32[]{:S(2)}, u32[]{:S(2)}) %collective-permute-start.7) | collective-permute-done | bytes 409632 | tf_op jit(solution)/shard_map/ppermute | solution.py:17
  95.8 5.8 %collective-permute-start.12 = (f32[160,640]{1,0:T(8,128)}, f32[160,640]{1,0:T(8,128)}, u32[]{:S(2)}, u32[]{:S(2)}) collective-permute-start(f32[160,640]{1,0:T(8,128)} %fusion.37), channel_id=1, source_target_pairs={{0,4},{4,8},{8,12},{12,16},{16,20},{20,24},{24,28},{1,5},{5,9},{9,... | collective-permute-start | bytes 1228808 | tf_op jit(solution)/shard_map/ppermute | solution.py:17
  101.6 3.1 %collective-permute-done.9 = f32[160,640]{1,0:T(8,128)} collective-permute-done((f32[160,640]{1,0:T(8,128)}, f32[160,640]{1,0:T(8,128)}, u32[]{:S(2)}, u32[]{:S(2)}) %collective-permute-start.9) | collective-permute-done | bytes 409632 | tf_op jit(solution)/shard_map/ppermute | solution.py:139
  104.7 3.5 %collective-permute-done.13 = f32[160,640]{1,0:T(8,128)S(1)} collective-permute-done((f32[160,640]{1,0:T(8,128)S(1)}, f32[160,640]{1,0:T(8,128)S(1)}, u32[]{:S(2)}, u32[]{:S(2)}) %collective-permute-start.13) | collective-permute-done | bytes 409632 | tf_op jit(solution)/shard_map/ppermute | solution.py:17
  109.8 7.5 %collective-permute-done.12 = f32[160,640]{1,0:T(8,128)} collective-permute-done((f32[160,640]{1,0:T(8,128)}, f32[160,640]{1,0:T(8,128)}, u32[]{:S(2)}, u32[]{:S(2)}) %collective-permute-start.12) | collective-permute-done | bytes 409632 | tf_op jit(solution)/shard_map/ppermute | solution.py:17
  117.3 2.6 %fusion.18 = f32[160,640]{1,0:T(8,128)} fusion(f32[160,640]{1,0:T(8,128)} %collective-permute-done.12, f32[160,640]{1,0:T(8,128)S(1)} %get-tuple-element.27, f32[160,640]{1,0:T(8,128)S(1)} %get-tuple-element.26, f32[160,640]{1,0:T(8,128)S(1)} %get-tuple-element.25, f32[160,640]{1,0:T(8,128)S(1)} %get-tuple-element.24), kind=kOutput, calls=%fused_computation.21 | convolution fusion | flops 394956800 | bytes 2457600 | tf_op jit(solution)/shard_map/dot_general | solution.py:21
  124.4 4.6 %collective-permute-start.16 = (f32[640,256]{1,0:T(8,128)S(1)}, f32[640,256]{1,0:T(8,128)S(1)}, u32[]{:S(2)}, u32[]{:S(2)}) collective-permute-start(f32[640,256]{1,0:T(8,128)S(1)} %fusion.31), channel_id=1, source_target_pairs={{0,4},{4,8},{8,12},{12,16},{16,20},{20,24},{24,28},{1,5},{5,9},{9,... | collective-permute-start | bytes 1966088 | tf_op jit(solution)/shard_map/ppermute | solution.py:17
  130.3 28.6 %invert.3 = f32[640,640]{1,0:T(8,128)S(1)} custom-call(f32[640,640]{1,0:T(8,128)S(1)} %pad_maximum_fusion.2.a_ref), custom_call_target="tpu_custom_call" | custom-call | flops 1572864000 | bytes 3276800 | tf_op jit(solution)/shard_map/invert/pallas_call | solution.py:125
  160.3 6.9 %collective-permute-start.14 = (f32[320,640]{1,0:T(8,128)S(1)}, f32[320,640]{1,0:T(8,128)}, u32[]{:S(2)}, u32[]{:S(2)}) collective-permute-start(f32[320,640]{1,0:T(8,128)S(1)} %fusion.21), channel_id=1, source_target_pairs={{0,8},{4,12},{8,16},{12,20},{16,24},{20,28},{1,9},{5,13},{9,17},{1... | collective-permute-start | bytes 2457608 | tf_op jit(solution)/shard_map/ppermute | solution.py:17
  174.9 6.0 %collective-permute-start.18 = (f32[640,256]{1,0:T(8,128)}, f32[640,256]{1,0:T(8,128)}, u32[]{:S(2)}, u32[]{:S(2)}) collective-permute-start(f32[640,256]{1,0:T(8,128)} %fusion.52), channel_id=1, source_target_pairs={{0,8},{4,12},{8,16},{12,20},{16,24},{20,28},{1,9},{5,13},{9,17},{1... | collective-permute-start | bytes 1966088 | tf_op jit(solution)/shard_map/ppermute | solution.py:17
  180.9 4.1 %collective-permute-done.14 = f32[320,640]{1,0:T(8,128)} collective-permute-done((f32[320,640]{1,0:T(8,128)S(1)}, f32[320,640]{1,0:T(8,128)}, u32[]{:S(2)}, u32[]{:S(2)}) %collective-permute-start.14) | collective-permute-done | bytes 819232 | tf_op jit(solution)/shard_map/ppermute | solution.py:17
  185.0 3.0 %fusion.50 = f32[320,640]{1,0:T(8,128)S(1)} fusion(f32[320,640]{1,0:T(8,128)} %collective-permute-done.14, f32[640,640]{1,0:T(8,128)} %all-gather.3.cloned.1.call-done), kind=kOutput, calls=%fused_computation.85 | convolution fusion | flops 786432000 | bytes 3276800 | tf_op jit(solution)/shard_map/dot_general | solution.py:21
  188.0 2.3 %collective-permute-done.15 = f32[320,640]{1,0:T(8,128)S(1)} collective-permute-done((f32[320,640]{1,0:T(8,128)S(1)}, f32[320,640]{1,0:T(8,128)S(1)}, u32[]{:S(2)}, u32[]{:S(2)}) %collective-permute-start.15) | collective-permute-done | bytes 819232 | tf_op jit(solution)/shard_map/ppermute | solution.py:17
  190.3 2.8 %fusion.51 = f32[320,640]{1,0:T(8,128)S(1)} fusion(f32[320,640]{1,0:T(8,128)S(1)} %collective-permute-done.15, f32[640,640]{1,0:T(8,128)} %all-gather.5.cloned.1.call-done), kind=kOutput, calls=%fused_computation.86 | convolution fusion | flops 786432000 | bytes 3276800 | tf_op jit(solution)/shard_map/dot_general | solution.py:21
  193.0 2.2 %fusion.33 = (f32[1,160,640]{2,1,0:T(8,128)}, f32[1,160,640]{2,1,0:T(8,128)}, f32[1,160,640]{2,1,0:T(8,128)}) fusion(f32[320,640]{1,0:T(8,128)S(1)} %fusion.51, f32[160,640]{1,0:T(8,128)} %subtract_subtract_fusion, f32[320,640]{1,0:T(8,128)S(1)} %fusion.50), kind=kLoop, calls=%fused_computation.35 | loop fusion | flops 409600 | bytes 3276800 | tf_op jit(solution)/shard_map/broadcast_in_dim | solution.py:215
  195.2 6.0 %collective-permute-done.19 = f32[640,256]{1,0:T(8,128)} collective-permute-done((f32[640,256]{1,0:T(8,128)}, f32[640,256]{1,0:T(8,128)}, u32[]{:S(2)}, u32[]{:S(2)}) %collective-permute-start.19) | collective-permute-done | bytes 655392 | tf_op jit(solution)/shard_map/ppermute | solution.py:17
  201.2 2.6 %fusion.53 = f32[640,256]{1,0:T(8,128)S(1)} fusion(f32[640,640]{1,0:T(8,128)S(1)} %copy-done.1, f32[640,256]{1,0:T(8,128)} %collective-permute-done.19), kind=kOutput, calls=%fused_computation.88 | convolution fusion | flops 629145600 | bytes 2949120 | tf_op jit(solution)/shard_map/dot_general | solution.py:25
  203.8 3.4 %fusion.13 = f32[1,640,256]{2,1,0:T(8,128)} fusion(f32[640,256]{1,0:T(8,128)S(1)} %fusion.53, f32[640,256]{1,0:T(8,128)S(1)} %fusion.9, f32[640,640]{1,0:T(8,128)S(1)} %copy-done, f32[640,256]{1,0:T(8,128)} %collective-permute-done.18), kind=kOutput, calls=%fused_computation.16 | convolution fusion | flops 629473280 | bytes 4259840 | tf_op jit(solution)/shard_map/dot_general | solution.py:25
  (100 shorter events, 35.6 us)
Async XLA Ops:
  7.2 177.8 %all-gather.3.cloned.1.call-start = ((), (), s32[]{:S(2)}) async-start(), calls=%async_computation | async-start | bytes 2048000 | tf_op jit(solution)/shard_map/all_gather | solution.py:197
  9.1 13.6 %collective-permute-start = (f32[160,640]{1,0:T(8,128)S(1)}, f32[160,640]{1,0:T(8,128)S(1)}, u32[]{:S(2)}, u32[]{:S(2)}) collective-permute-start(f32[160,640]{1,0:T(8,128)S(1)} %fusion.36), channel_id=1, source_target_pairs={{0,4},{4,8},{8,12},{12,16},{16,20},{20,24},{24,28},{1,5},{5,9},{9,... | collective-permute-start | bytes 1228808 | tf_op jit(solution)/shard_map/ppermute | solution.py:17
  14.0 11.7 %collective-permute-start.4 = (f32[160,640]{1,0:T(8,128)S(1)}, f32[160,640]{1,0:T(8,128)S(1)}, u32[]{:S(2)}, u32[]{:S(2)}) collective-permute-start(f32[160,640]{1,0:T(8,128)S(1)} %fusion.36), channel_id=1, source_target_pairs={{0,2},{1,3},{2,0},{3,1},{4,6},{5,7},{6,4},{7,5},{8,10},{9,11},{10,... | collective-permute-start | bytes 1228808 | tf_op jit(solution)/shard_map/ppermute | solution.py:139
  22.7 11.1 %collective-permute-start.1 = (f32[160,640]{1,0:T(8,128)S(1)}, f32[160,640]{1,0:T(8,128)S(1)}, u32[]{:S(2)}, u32[]{:S(2)}) collective-permute-start(f32[160,640]{1,0:T(8,128)S(1)} %collective-permute-done), channel_id=1, source_target_pairs={{0,2},{1,3},{2,0},{3,1},{4,6},{5,7},{6,4},{7,5},{8,10},{9,11},{10,... | collective-permute-start | bytes 1228808 | tf_op jit(solution)/shard_map/ppermute | solution.py:139
  24.2 10.3 %collective-permute-start.6 = (f32[160,640]{1,0:T(8,128)S(1)}, f32[160,640]{1,0:T(8,128)S(1)}, u32[]{:S(2)}, u32[]{:S(2)}) collective-permute-start(f32[160,640]{1,0:T(8,128)S(1)} %fusion.36), channel_id=1, source_target_pairs={{0,1},{1,0},{2,3},{3,2},{4,5},{5,4},{6,7},{7,6},{8,9},{9,8},{10,11... | collective-permute-start | bytes 1228808 | tf_op jit(solution)/shard_map/ppermute | solution.py:139
  25.7 8.8 %collective-permute-start.5 = (f32[160,640]{1,0:T(8,128)S(1)}, f32[160,640]{1,0:T(8,128)S(1)}, u32[]{:S(2)}, u32[]{:S(2)}) collective-permute-start(f32[160,640]{1,0:T(8,128)S(1)} %collective-permute-done.4), channel_id=1, source_target_pairs={{0,1},{1,0},{2,3},{3,2},{4,5},{5,4},{6,7},{7,6},{8,9},{9,8},{10,11... | collective-permute-start | bytes 1228808 | tf_op jit(solution)/shard_map/ppermute | solution.py:139
  25.7 10.1 %collective-permute-start.3 = (f32[160,640]{1,0:T(8,128)S(1)}, f32[160,640]{1,0:T(8,128)S(1)}, u32[]{:S(2)}, u32[]{:S(2)}) collective-permute-start(f32[160,640]{1,0:T(8,128)S(1)} %collective-permute-done), channel_id=1, source_target_pairs={{0,1},{1,0},{2,3},{3,2},{4,5},{5,4},{6,7},{7,6},{8,9},{9,8},{10,11... | collective-permute-start | bytes 1228808 | tf_op jit(solution)/shard_map/ppermute | solution.py:139
  33.8 2.0 collective-permute-start.2
  37.3 80.0 %copy-start.2 = (f32[160,640]{1,0:T(8,128)}, f32[160,640]{1,0:T(8,128)S(1)}, u32[]{:S(2)}) copy-start(f32[160,640]{1,0:T(8,128)S(1)} %get-tuple-element.24) | copy-start | bytes 1228804
  37.3 80.0 %copy-start.4 = (f32[160,640]{1,0:T(8,128)}, f32[160,640]{1,0:T(8,128)S(1)}, u32[]{:S(2)}) copy-start(f32[160,640]{1,0:T(8,128)S(1)} %get-tuple-element.25) | copy-start | bytes 1228804
  67.7 14.0 %collective-permute-start.8 = (f32[160,640]{1,0:T(8,128)}, f32[160,640]{1,0:T(8,128)S(1)}, u32[]{:S(2)}, u32[]{:S(2)}) collective-permute-start(f32[160,640]{1,0:T(8,128)} %fusion.37), channel_id=1, source_target_pairs={{4,0},{8,4},{12,8},{16,12},{20,16},{24,20},{28,24},{5,1},{9,5},{13... | collective-permute-start | bytes 1228808 | tf_op jit(solution)/shard_map/ppermute | solution.py:17
  69.7 20.8 %collective-permute-start.7 = (f32[160,640]{1,0:T(8,128)S(1)}, f32[160,640]{1,0:T(8,128)S(1)}, u32[]{:S(2)}, u32[]{:S(2)}) collective-permute-start(f32[160,640]{1,0:T(8,128)S(1)} %fusion.39), channel_id=1, source_target_pairs={{0,4},{4,8},{8,12},{12,16},{16,20},{20,24},{24,28},{1,5},{5,9},{9,... | collective-permute-start | bytes 1228808 | tf_op jit(solution)/shard_map/ppermute | solution.py:17
  93.0 11.7 %collective-permute-start.9 = (f32[160,640]{1,0:T(8,128)}, f32[160,640]{1,0:T(8,128)}, u32[]{:S(2)}, u32[]{:S(2)}) collective-permute-start(f32[160,640]{1,0:T(8,128)} %subtract_subtract_fusion), channel_id=1, source_target_pairs={{0,2},{1,3},{2,0},{3,1},{4,6},{5,7},{6,4},{7,5},{8,10},{9,11},{10,... | collective-permute-start | bytes 1228808 | tf_op jit(solution)/shard_map/ppermute | solution.py:139
  94.5 13.8 %collective-permute-start.13 = (f32[160,640]{1,0:T(8,128)S(1)}, f32[160,640]{1,0:T(8,128)S(1)}, u32[]{:S(2)}, u32[]{:S(2)}) collective-permute-start(f32[160,640]{1,0:T(8,128)S(1)} %fusion.39), channel_id=1, source_target_pairs={{4,0},{8,4},{12,8},{16,12},{20,16},{24,20},{28,24},{5,1},{9,5},{13... | collective-permute-start | bytes 1228808 | tf_op jit(solution)/shard_map/ppermute | solution.py:17
  95.8 21.5 %collective-permute-start.12 = (f32[160,640]{1,0:T(8,128)}, f32[160,640]{1,0:T(8,128)}, u32[]{:S(2)}, u32[]{:S(2)}) collective-permute-start(f32[160,640]{1,0:T(8,128)} %fusion.37), channel_id=1, source_target_pairs={{0,4},{4,8},{8,12},{12,16},{16,20},{20,24},{24,28},{1,5},{5,9},{9,... | collective-permute-start | bytes 1228808 | tf_op jit(solution)/shard_map/ppermute | solution.py:17
  101.6 18.4 %collective-permute-start.11 = (f32[160,640]{1,0:T(8,128)}, f32[160,640]{1,0:T(8,128)}, u32[]{:S(2)}, u32[]{:S(2)}) collective-permute-start(f32[160,640]{1,0:T(8,128)} %subtract_subtract_fusion), channel_id=1, source_target_pairs={{0,1},{1,0},{2,3},{3,2},{4,5},{5,4},{6,7},{7,6},{8,9},{9,8},{10,11... | collective-permute-start | bytes 1228808 | tf_op jit(solution)/shard_map/ppermute | solution.py:139
  104.7 15.2 %collective-permute-start.10 = (f32[160,640]{1,0:T(8,128)}, f32[160,640]{1,0:T(8,128)}, u32[]{:S(2)}, u32[]{:S(2)}) collective-permute-start(f32[160,640]{1,0:T(8,128)} %collective-permute-done.9), channel_id=1, source_target_pairs={{0,1},{1,0},{2,3},{3,2},{4,5},{5,4},{6,7},{7,6},{8,9},{9,8},{10,11... | collective-permute-start | bytes 1228808 | tf_op jit(solution)/shard_map/ppermute | solution.py:139
  121.6 68.6 %all-gather.5.cloned.1.call-start = ((), (), s32[]{:S(2)}) async-start(), calls=%async_computation.1 | async-start | bytes 2048000 | tf_op jit(solution)/shard_map/all_gather | solution.py:198
  124.4 44.3 %collective-permute-start.16 = (f32[640,256]{1,0:T(8,128)S(1)}, f32[640,256]{1,0:T(8,128)S(1)}, u32[]{:S(2)}, u32[]{:S(2)}) collective-permute-start(f32[640,256]{1,0:T(8,128)S(1)} %fusion.31), channel_id=1, source_target_pairs={{0,4},{4,8},{8,12},{12,16},{16,20},{20,24},{24,28},{1,5},{5,9},{9,... | collective-permute-start | bytes 1966088 | tf_op jit(solution)/shard_map/ppermute | solution.py:17
  129.0 39.7 %collective-permute-start.17 = (f32[640,256]{1,0:T(8,128)S(1)}, f32[640,256]{1,0:T(8,128)S(1)}, u32[]{:S(2)}, u32[]{:S(2)}) collective-permute-start(f32[640,256]{1,0:T(8,128)S(1)} %fusion.31), channel_id=1, source_target_pairs={{4,0},{8,4},{12,8},{16,12},{20,16},{24,20},{28,24},{5,1},{9,5},{13... | collective-permute-start | bytes 1966088 | tf_op jit(solution)/shard_map/ppermute | solution.py:17
  160.3 24.7 %collective-permute-start.14 = (f32[320,640]{1,0:T(8,128)S(1)}, f32[320,640]{1,0:T(8,128)}, u32[]{:S(2)}, u32[]{:S(2)}) collective-permute-start(f32[320,640]{1,0:T(8,128)S(1)} %fusion.21), channel_id=1, source_target_pairs={{0,8},{4,12},{8,16},{12,20},{16,24},{20,28},{1,9},{5,13},{9,17},{1... | collective-permute-start | bytes 2457608 | tf_op jit(solution)/shard_map/ppermute | solution.py:17
  167.2 23.1 %collective-permute-start.15 = (f32[320,640]{1,0:T(8,128)S(1)}, f32[320,640]{1,0:T(8,128)S(1)}, u32[]{:S(2)}, u32[]{:S(2)}) collective-permute-start(f32[320,640]{1,0:T(8,128)S(1)} %fusion.21), channel_id=1, source_target_pairs={{8,0},{12,4},{16,8},{20,12},{24,16},{28,20},{9,1},{13,5},{17,9},{2... | collective-permute-start | bytes 2457608 | tf_op jit(solution)/shard_map/ppermute | solution.py:17
  173.6 27.6 %collective-permute-start.19 = (f32[640,256]{1,0:T(8,128)}, f32[640,256]{1,0:T(8,128)}, u32[]{:S(2)}, u32[]{:S(2)}) collective-permute-start(f32[640,256]{1,0:T(8,128)} %fusion.52), channel_id=1, source_target_pairs={{8,0},{12,4},{16,8},{20,12},{24,16},{28,20},{9,1},{13,5},{17,9},{2... | collective-permute-start | bytes 1966088 | tf_op jit(solution)/shard_map/ppermute | solution.py:17
  174.9 28.9 %collective-permute-start.18 = (f32[640,256]{1,0:T(8,128)}, f32[640,256]{1,0:T(8,128)}, u32[]{:S(2)}, u32[]{:S(2)}) collective-permute-start(f32[640,256]{1,0:T(8,128)} %fusion.52), channel_id=1, source_target_pairs={{0,8},{4,12},{8,16},{12,20},{16,24},{20,28},{1,9},{5,13},{9,17},{1... | collective-permute-start | bytes 1966088 | tf_op jit(solution)/shard_map/ppermute | solution.py:17
  (23 other events, 696.1 us)
Sparse Core Ops, SparseCore 0:
  121.7 20.6 all-gather.2
  144.5 20.0 all-gather.4

commit v3 on v2

--- a/solution.py
+++ b/solution.py
@@ -70,6 +70,11 @@
     return rows
 
 
+def halves(x):
+    high = x.astype(BF16).astype(F32)
+    return high, x - high
+
+
 def block_inverses(blocks):
     count = BLOCK // LEAF
     rows = lax.broadcasted_iota(jnp.int32, (LEAF, BLOCK), 0)
@@ -85,16 +90,27 @@
             entries = {(i, j): sub(columns[j], i) for j in range(LEAF) for i in range(j + 1)}
             framed = jnp.where(inside, unit, row)
             steps = eliminate(entries, [sub(framed, j) for j in range(LEAF)])
-            order = list(range(t + 1, count)) + list(range(t))
-            for s in order:
-                old = held[s]
-                total = jnp.where(inside, 0.0, old)
-                for j in range(LEAF):
-                    total = total - spread(old, base + j) * steps[j]
-                held[s] = total
             new = steps[0]
             for j in range(1, LEAF):
                 new = jnp.where(rows == j, steps[j], new)
+            high, low = halves(jnp.where(inside, 0.0, jnp.where(lanes < base, -row, row)))
+            new_high, new_low = halves(new)
+            update = lax.dot_general(
+                jnp.concatenate([high, low, high, low], axis=0).astype(BF16),
+                jnp.concatenate([new_high, new_high, new_low, new_low], axis=0).astype(BF16),
+                (((0,), (0,)), ((), ())),
+                preferred_element_type=F32,
+            )
+            for s in range(count):
+                if s == t:
+                    continue
+                total = jnp.where(inside, 0.0, held[s])
+                if s == t + 1:
+                    for j in range(LEAF):
+                        total = total - spread(held[s], base + j) * steps[j]
+                else:
+                    total = total - update[LEAF * s : LEAF * (s + 1), :]
+                held[s] = total
             held[t] = new
     return [jnp.concatenate(held, axis=0) for held in tiles]
 

time: 215 us -> 204 us (0.949)
  Pallas kernels: 57.2 us -> 46.2 us
    pallas_call x2, Pallas kernels: 57.2 us -> 46.2 us  [invert(): pl.pallas_call(invert_kernel, out_shape=jax.ShapeDtypeStruct((size, size)...]
  transfers between devices with their start and end apart: 22 -> 22, of which waited for: 11 -> 11; matrix products, arithmetic and copies ran while one was open for 12% -> 13% of each run, Pallas kernels for 13% -> 11%
where the time goes in v3:
time: 204 us; the launch traced here: 203 us
  waiting for transfers between devices  59.8 us (29%)
  Pallas kernels  46.2 us (23%)
  starting transfers between devices  44.5 us (22%)
  matrix products  28.8 us (14%)
  between operations  14.6 us (7%)
  other arithmetic  9.15 us (4%)
    ppermute x11, waiting for transfers between devices, from_behind(): return lax.ppermute(shard, axis, pairs)  46.9 us
    pallas_call x2, Pallas kernels, invert(): pl.pallas_call(invert_kernel, out_shape=jax.ShapeDtypeStruct((size, size)...  46.2 us
    ppermute x11, starting transfers between devices, from_behind(): return lax.ppermute(shard, axis, pairs)  39.3 us
    dot_general x11, matrix products, matmul(): jnp.dot(left, right, precision=lax.Precision.HIGH, preferred_element_type...  19.9 us
    ppermute x9, waiting for transfers between devices, gather(): swap = lambda x, by: lax.ppermute(x, 'rhs', [(i, i ^ by) for i in range(4)])  12.2 us
    dot_general x4, matrix products, leading_matmul(): lax.dot_general(left, right, (((0,), (0,)), ((), ())), precision=lax.Prec...  8.96 us
    ppermute x9, starting transfers between devices, gather(): swap = lambda x, by: lax.ppermute(x, 'rhs', [(i, i ^ by) for i in range(4)])  5.06 us
    select_n x3, other arithmetic, gather(): jnp.where(high, pair[1], pair[0])  4.16 us
  transfers between devices with their start and end apart: 22, of which 11 were waited for; matrix products, arithmetic and copies ran while one was open for 13% of the time, Pallas kernels for 11%

profile of v3, /device:TPU:0, one launch (start us, length us, event | category | flops | bytes accessed | tf_op | source)
XLA Modules:
  0.0 203.3 jit_solution(4686746694195658804)
XLA Ops:
  9.1 4.9 %collective-permute-start = (f32[160,640]{1,0:T(8,128)S(1)}, f32[160,640]{1,0:T(8,128)S(1)}, u32[]{:S(2)}, u32[]{:S(2)}) collective-permute-start(f32[160,640]{1,0:T(8,128)S(1)} %fusion.36), channel_id=1, source_target_pairs={{0,4},{4,8},{8,12},{12,16},{16,20},{20,24},{24,28},{1,5},{5,9},{9,... | collective-permute-start | bytes 1228808 | tf_op jit(solution)/shard_map/ppermute | solution.py:17
  15.6 7.1 %collective-permute-done = f32[160,640]{1,0:T(8,128)S(1)} collective-permute-done((f32[160,640]{1,0:T(8,128)S(1)}, f32[160,640]{1,0:T(8,128)S(1)}, u32[]{:S(2)}, u32[]{:S(2)}) %collective-permute-start) | collective-permute-done | bytes 409632 | tf_op jit(solution)/shard_map/ppermute | solution.py:17
  26.2 7.6 %collective-permute-done.1 = f32[160,640]{1,0:T(8,128)S(1)} collective-permute-done((f32[160,640]{1,0:T(8,128)S(1)}, f32[160,640]{1,0:T(8,128)S(1)}, u32[]{:S(2)}, u32[]{:S(2)}) %collective-permute-start.1) | collective-permute-done | bytes 409632 | tf_op jit(solution)/shard_map/ppermute | solution.py:155
  37.5 23.1 %invert.2 = f32[640,640]{1,0:T(8,128)S(1)} custom-call(f32[640,640]{1,0:T(8,128)S(1)} %select_add_fusion.a_ref), custom_call_target="tpu_custom_call" | custom-call | flops 1572864000 | bytes 3276800 | tf_op jit(solution)/shard_map/invert/pallas_call | solution.py:141
  64.3 4.6 %collective-permute-start.7 = (f32[160,640]{1,0:T(8,128)S(1)}, f32[160,640]{1,0:T(8,128)S(1)}, u32[]{:S(2)}, u32[]{:S(2)}) collective-permute-start(f32[160,640]{1,0:T(8,128)S(1)} %fusion.39), channel_id=1, source_target_pairs={{0,4},{4,8},{8,12},{12,16},{16,20},{20,24},{24,28},{1,5},{5,9},{9,... | collective-permute-start | bytes 1228808 | tf_op jit(solution)/shard_map/ppermute | solution.py:17
  68.9 7.3 %collective-permute-done.8 = f32[160,640]{1,0:T(8,128)S(1)} collective-permute-done((f32[160,640]{1,0:T(8,128)}, f32[160,640]{1,0:T(8,128)S(1)}, u32[]{:S(2)}, u32[]{:S(2)}) %collective-permute-start.8) | collective-permute-done | bytes 409632 | tf_op jit(solution)/shard_map/ppermute | solution.py:17
  76.2 8.9 %collective-permute-done.7 = f32[160,640]{1,0:T(8,128)S(1)} collective-permute-done((f32[160,640]{1,0:T(8,128)S(1)}, f32[160,640]{1,0:T(8,128)S(1)}, u32[]{:S(2)}, u32[]{:S(2)}) %collective-permute-start.7) | collective-permute-done | bytes 409632 | tf_op jit(solution)/shard_map/ppermute | solution.py:17
  90.3 5.8 %collective-permute-start.12 = (f32[160,640]{1,0:T(8,128)}, f32[160,640]{1,0:T(8,128)}, u32[]{:S(2)}, u32[]{:S(2)}) collective-permute-start(f32[160,640]{1,0:T(8,128)} %fusion.37), channel_id=1, source_target_pairs={{0,4},{4,8},{8,12},{12,16},{16,20},{20,24},{24,28},{1,5},{5,9},{9,... | collective-permute-start | bytes 1228808 | tf_op jit(solution)/shard_map/ppermute | solution.py:17
  96.1 3.1 %collective-permute-done.9 = f32[160,640]{1,0:T(8,128)} collective-permute-done((f32[160,640]{1,0:T(8,128)}, f32[160,640]{1,0:T(8,128)}, u32[]{:S(2)}, u32[]{:S(2)}) %collective-permute-start.9) | collective-permute-done | bytes 409632 | tf_op jit(solution)/shard_map/ppermute | solution.py:155
  99.3 3.5 %collective-permute-done.13 = f32[160,640]{1,0:T(8,128)S(1)} collective-permute-done((f32[160,640]{1,0:T(8,128)S(1)}, f32[160,640]{1,0:T(8,128)S(1)}, u32[]{:S(2)}, u32[]{:S(2)}) %collective-permute-start.13) | collective-permute-done | bytes 409632 | tf_op jit(solution)/shard_map/ppermute | solution.py:17
  104.4 7.5 %collective-permute-done.12 = f32[160,640]{1,0:T(8,128)} collective-permute-done((f32[160,640]{1,0:T(8,128)}, f32[160,640]{1,0:T(8,128)}, u32[]{:S(2)}, u32[]{:S(2)}) %collective-permute-start.12) | collective-permute-done | bytes 409632 | tf_op jit(solution)/shard_map/ppermute | solution.py:17
  111.8 2.6 %fusion.18 = f32[160,640]{1,0:T(8,128)} fusion(f32[160,640]{1,0:T(8,128)} %collective-permute-done.12, f32[160,640]{1,0:T(8,128)S(1)} %get-tuple-element.27, f32[160,640]{1,0:T(8,128)S(1)} %get-tuple-element.26, f32[160,640]{1,0:T(8,128)S(1)} %get-tuple-element.25, f32[160,640]{1,0:T(8,128)S(1)} %get-tuple-element.24), kind=kOutput, calls=%fused_computation.21 | convolution fusion | flops 394956800 | bytes 2457600 | tf_op jit(solution)/shard_map/dot_general | solution.py:21
  119.0 4.7 %collective-permute-start.16 = (f32[640,256]{1,0:T(8,128)S(1)}, f32[640,256]{1,0:T(8,128)S(1)}, u32[]{:S(2)}, u32[]{:S(2)}) collective-permute-start(f32[640,256]{1,0:T(8,128)S(1)} %fusion.31), channel_id=1, source_target_pairs={{0,4},{4,8},{8,12},{12,16},{16,20},{20,24},{24,28},{1,5},{5,9},{9,... | collective-permute-start | bytes 1966088 | tf_op jit(solution)/shard_map/ppermute | solution.py:17
  125.0 23.1 %invert.3 = f32[640,640]{1,0:T(8,128)S(1)} custom-call(f32[640,640]{1,0:T(8,128)S(1)} %pad_maximum_fusion.2.a_ref), custom_call_target="tpu_custom_call" | custom-call | flops 1572864000 | bytes 3276800 | tf_op jit(solution)/shard_map/invert/pallas_call | solution.py:141
  149.6 6.9 %collective-permute-start.14 = (f32[320,640]{1,0:T(8,128)S(1)}, f32[320,640]{1,0:T(8,128)}, u32[]{:S(2)}, u32[]{:S(2)}) collective-permute-start(f32[320,640]{1,0:T(8,128)S(1)} %fusion.21), channel_id=1, source_target_pairs={{0,8},{4,12},{8,16},{12,20},{16,24},{20,28},{1,9},{5,13},{9,17},{1... | collective-permute-start | bytes 2457608 | tf_op jit(solution)/shard_map/ppermute | solution.py:17
  163.9 6.0 %collective-permute-start.18 = (f32[640,256]{1,0:T(8,128)}, f32[640,256]{1,0:T(8,128)}, u32[]{:S(2)}, u32[]{:S(2)}) collective-permute-start(f32[640,256]{1,0:T(8,128)} %fusion.52), channel_id=1, source_target_pairs={{0,8},{4,12},{8,16},{12,20},{16,24},{20,28},{1,9},{5,13},{9,17},{1... | collective-permute-start | bytes 1966088 | tf_op jit(solution)/shard_map/ppermute | solution.py:17
  169.9 4.3 %collective-permute-done.14 = f32[320,640]{1,0:T(8,128)} collective-permute-done((f32[320,640]{1,0:T(8,128)S(1)}, f32[320,640]{1,0:T(8,128)}, u32[]{:S(2)}, u32[]{:S(2)}) %collective-permute-start.14) | collective-permute-done | bytes 819232 | tf_op jit(solution)/shard_map/ppermute | solution.py:17
  174.2 3.0 %fusion.50 = f32[320,640]{1,0:T(8,128)S(1)} fusion(f32[320,640]{1,0:T(8,128)} %collective-permute-done.14, f32[640,640]{1,0:T(8,128)} %all-gather.3.cloned.1.call-done), kind=kOutput, calls=%fused_computation.85 | convolution fusion | flops 786432000 | bytes 3276800 | tf_op jit(solution)/shard_map/dot_general | solution.py:21
  177.2 2.3 %collective-permute-done.15 = f32[320,640]{1,0:T(8,128)S(1)} collective-permute-done((f32[320,640]{1,0:T(8,128)S(1)}, f32[320,640]{1,0:T(8,128)S(1)}, u32[]{:S(2)}, u32[]{:S(2)}) %collective-permute-start.15) | collective-permute-done | bytes 819232 | tf_op jit(solution)/shard_map/ppermute | solution.py:17
  179.5 2.8 %fusion.51 = f32[320,640]{1,0:T(8,128)S(1)} fusion(f32[320,640]{1,0:T(8,128)S(1)} %collective-permute-done.15, f32[640,640]{1,0:T(8,128)} %all-gather.5.cloned.1.call-done), kind=kOutput, calls=%fused_computation.86 | convolution fusion | flops 786432000 | bytes 3276800 | tf_op jit(solution)/shard_map/dot_general | solution.py:21
  182.3 2.2 %fusion.33 = (f32[1,160,640]{2,1,0:T(8,128)}, f32[1,160,640]{2,1,0:T(8,128)}, f32[1,160,640]{2,1,0:T(8,128)}) fusion(f32[320,640]{1,0:T(8,128)S(1)} %fusion.51, f32[160,640]{1,0:T(8,128)} %subtract_subtract_fusion, f32[320,640]{1,0:T(8,128)S(1)} %fusion.50), kind=kLoop, calls=%fused_computation.35 | loop fusion | flops 409600 | bytes 3276800 | tf_op jit(solution)/shard_map/broadcast_in_dim | solution.py:231
  184.5 6.0 %collective-permute-done.19 = f32[640,256]{1,0:T(8,128)} collective-permute-done((f32[640,256]{1,0:T(8,128)}, f32[640,256]{1,0:T(8,128)}, u32[]{:S(2)}, u32[]{:S(2)}) %collective-permute-start.19) | collective-permute-done | bytes 655392 | tf_op jit(solution)/shard_map/ppermute | solution.py:17
  190.4 2.6 %fusion.53 = f32[640,256]{1,0:T(8,128)S(1)} fusion(f32[640,640]{1,0:T(8,128)S(1)} %copy-done.1, f32[640,256]{1,0:T(8,128)} %collective-permute-done.19), kind=kOutput, calls=%fused_computation.88 | convolution fusion | flops 629145600 | bytes 2949120 | tf_op jit(solution)/shard_map/dot_general | solution.py:25
  193.0 3.4 %fusion.13 = f32[1,640,256]{2,1,0:T(8,128)} fusion(f32[640,256]{1,0:T(8,128)S(1)} %fusion.53, f32[640,256]{1,0:T(8,128)S(1)} %fusion.9, f32[640,640]{1,0:T(8,128)S(1)} %copy-done, f32[640,256]{1,0:T(8,128)} %collective-permute-done.18), kind=kOutput, calls=%fused_computation.16 | convolution fusion | flops 629473280 | bytes 4259840 | tf_op jit(solution)/shard_map/dot_general | solution.py:25
  (100 shorter events, 35.4 us)
Async XLA Ops:
  7.2 167.1 %all-gather.3.cloned.1.call-start = ((), (), s32[]{:S(2)}) async-start(), calls=%async_computation | async-start | bytes 2048000 | tf_op jit(solution)/shard_map/all_gather | solution.py:213
  9.1 13.6 %collective-permute-start = (f32[160,640]{1,0:T(8,128)S(1)}, f32[160,640]{1,0:T(8,128)S(1)}, u32[]{:S(2)}, u32[]{:S(2)}) collective-permute-start(f32[160,640]{1,0:T(8,128)S(1)} %fusion.36), channel_id=1, source_target_pairs={{0,4},{4,8},{8,12},{12,16},{16,20},{20,24},{24,28},{1,5},{5,9},{9,... | collective-permute-start | bytes 1228808 | tf_op jit(solution)/shard_map/ppermute | solution.py:17
  14.0 11.7 %collective-permute-start.4 = (f32[160,640]{1,0:T(8,128)S(1)}, f32[160,640]{1,0:T(8,128)S(1)}, u32[]{:S(2)}, u32[]{:S(2)}) collective-permute-start(f32[160,640]{1,0:T(8,128)S(1)} %fusion.36), channel_id=1, source_target_pairs={{0,2},{1,3},{2,0},{3,1},{4,6},{5,7},{6,4},{7,5},{8,10},{9,11},{10,... | collective-permute-start | bytes 1228808 | tf_op jit(solution)/shard_map/ppermute | solution.py:155
  22.7 11.1 %collective-permute-start.1 = (f32[160,640]{1,0:T(8,128)S(1)}, f32[160,640]{1,0:T(8,128)S(1)}, u32[]{:S(2)}, u32[]{:S(2)}) collective-permute-start(f32[160,640]{1,0:T(8,128)S(1)} %collective-permute-done), channel_id=1, source_target_pairs={{0,2},{1,3},{2,0},{3,1},{4,6},{5,7},{6,4},{7,5},{8,10},{9,11},{10,... | collective-permute-start | bytes 1228808 | tf_op jit(solution)/shard_map/ppermute | solution.py:155
  24.2 10.3 %collective-permute-start.6 = (f32[160,640]{1,0:T(8,128)S(1)}, f32[160,640]{1,0:T(8,128)S(1)}, u32[]{:S(2)}, u32[]{:S(2)}) collective-permute-start(f32[160,640]{1,0:T(8,128)S(1)} %fusion.36), channel_id=1, source_target_pairs={{0,1},{1,0},{2,3},{3,2},{4,5},{5,4},{6,7},{7,6},{8,9},{9,8},{10,11... | collective-permute-start | bytes 1228808 | tf_op jit(solution)/shard_map/ppermute | solution.py:155
  25.7 8.8 %collective-permute-start.5 = (f32[160,640]{1,0:T(8,128)S(1)}, f32[160,640]{1,0:T(8,128)S(1)}, u32[]{:S(2)}, u32[]{:S(2)}) collective-permute-start(f32[160,640]{1,0:T(8,128)S(1)} %collective-permute-done.4), channel_id=1, source_target_pairs={{0,1},{1,0},{2,3},{3,2},{4,5},{5,4},{6,7},{7,6},{8,9},{9,8},{10,11... | collective-permute-start | bytes 1228808 | tf_op jit(solution)/shard_map/ppermute | solution.py:155
  25.7 10.1 %collective-permute-start.3 = (f32[160,640]{1,0:T(8,128)S(1)}, f32[160,640]{1,0:T(8,128)S(1)}, u32[]{:S(2)}, u32[]{:S(2)}) collective-permute-start(f32[160,640]{1,0:T(8,128)S(1)} %collective-permute-done), channel_id=1, source_target_pairs={{0,1},{1,0},{2,3},{3,2},{4,5},{5,4},{6,7},{7,6},{8,9},{9,8},{10,11... | collective-permute-start | bytes 1228808 | tf_op jit(solution)/shard_map/ppermute | solution.py:155
  33.8 2.0 collective-permute-start.2
  37.3 74.6 %copy-start.2 = (f32[160,640]{1,0:T(8,128)}, f32[160,640]{1,0:T(8,128)S(1)}, u32[]{:S(2)}) copy-start(f32[160,640]{1,0:T(8,128)S(1)} %get-tuple-element.24) | copy-start | bytes 1228804
  37.3 74.6 %copy-start.4 = (f32[160,640]{1,0:T(8,128)}, f32[160,640]{1,0:T(8,128)S(1)}, u32[]{:S(2)}) copy-start(f32[160,640]{1,0:T(8,128)S(1)} %get-tuple-element.25) | copy-start | bytes 1228804
  62.2 14.0 %collective-permute-start.8 = (f32[160,640]{1,0:T(8,128)}, f32[160,640]{1,0:T(8,128)S(1)}, u32[]{:S(2)}, u32[]{:S(2)}) collective-permute-start(f32[160,640]{1,0:T(8,128)} %fusion.37), channel_id=1, source_target_pairs={{4,0},{8,4},{12,8},{16,12},{20,16},{24,20},{28,24},{5,1},{9,5},{13... | collective-permute-start | bytes 1228808 | tf_op jit(solution)/shard_map/ppermute | solution.py:17
  64.3 20.8 %collective-permute-start.7 = (f32[160,640]{1,0:T(8,128)S(1)}, f32[160,640]{1,0:T(8,128)S(1)}, u32[]{:S(2)}, u32[]{:S(2)}) collective-permute-start(f32[160,640]{1,0:T(8,128)S(1)} %fusion.39), channel_id=1, source_target_pairs={{0,4},{4,8},{8,12},{12,16},{16,20},{20,24},{24,28},{1,5},{5,9},{9,... | collective-permute-start | bytes 1228808 | tf_op jit(solution)/shard_map/ppermute | solution.py:17
  87.5 11.7 %collective-permute-start.9 = (f32[160,640]{1,0:T(8,128)}, f32[160,640]{1,0:T(8,128)}, u32[]{:S(2)}, u32[]{:S(2)}) collective-permute-start(f32[160,640]{1,0:T(8,128)} %subtract_subtract_fusion), channel_id=1, source_target_pairs={{0,2},{1,3},{2,0},{3,1},{4,6},{5,7},{6,4},{7,5},{8,10},{9,11},{10,... | collective-permute-start | bytes 1228808 | tf_op jit(solution)/shard_map/ppermute | solution.py:155
  89.0 13.8 %collective-permute-start.13 = (f32[160,640]{1,0:T(8,128)S(1)}, f32[160,640]{1,0:T(8,128)S(1)}, u32[]{:S(2)}, u32[]{:S(2)}) collective-permute-start(f32[160,640]{1,0:T(8,128)S(1)} %fusion.39), channel_id=1, source_target_pairs={{4,0},{8,4},{12,8},{16,12},{20,16},{24,20},{28,24},{5,1},{9,5},{13... | collective-permute-start | bytes 1228808 | tf_op jit(solution)/shard_map/ppermute | solution.py:17
  90.3 21.5 %collective-permute-start.12 = (f32[160,640]{1,0:T(8,128)}, f32[160,640]{1,0:T(8,128)}, u32[]{:S(2)}, u32[]{:S(2)}) collective-permute-start(f32[160,640]{1,0:T(8,128)} %fusion.37), channel_id=1, source_target_pairs={{0,4},{4,8},{8,12},{12,16},{16,20},{20,24},{24,28},{1,5},{5,9},{9,... | collective-permute-start | bytes 1228808 | tf_op jit(solution)/shard_map/ppermute | solution.py:17
  96.1 18.4 %collective-permute-start.11 = (f32[160,640]{1,0:T(8,128)}, f32[160,640]{1,0:T(8,128)}, u32[]{:S(2)}, u32[]{:S(2)}) collective-permute-start(f32[160,640]{1,0:T(8,128)} %subtract_subtract_fusion), channel_id=1, source_target_pairs={{0,1},{1,0},{2,3},{3,2},{4,5},{5,4},{6,7},{7,6},{8,9},{9,8},{10,11... | collective-permute-start | bytes 1228808 | tf_op jit(solution)/shard_map/ppermute | solution.py:155
  99.3 15.2 %collective-permute-start.10 = (f32[160,640]{1,0:T(8,128)}, f32[160,640]{1,0:T(8,128)}, u32[]{:S(2)}, u32[]{:S(2)}) collective-permute-start(f32[160,640]{1,0:T(8,128)} %collective-permute-done.9), channel_id=1, source_target_pairs={{0,1},{1,0},{2,3},{3,2},{4,5},{5,4},{6,7},{7,6},{8,9},{9,8},{10,11... | collective-permute-start | bytes 1228808 | tf_op jit(solution)/shard_map/ppermute | solution.py:155
  116.1 63.3 %all-gather.5.cloned.1.call-start = ((), (), s32[]{:S(2)}) async-start(), calls=%async_computation.1 | async-start | bytes 2048000 | tf_op jit(solution)/shard_map/all_gather | solution.py:214
  119.0 38.8 %collective-permute-start.16 = (f32[640,256]{1,0:T(8,128)S(1)}, f32[640,256]{1,0:T(8,128)S(1)}, u32[]{:S(2)}, u32[]{:S(2)}) collective-permute-start(f32[640,256]{1,0:T(8,128)S(1)} %fusion.31), channel_id=1, source_target_pairs={{0,4},{4,8},{8,12},{12,16},{16,20},{20,24},{24,28},{1,5},{5,9},{9,... | collective-permute-start | bytes 1966088 | tf_op jit(solution)/shard_map/ppermute | solution.py:17
  123.7 34.0 %collective-permute-start.17 = (f32[640,256]{1,0:T(8,128)S(1)}, f32[640,256]{1,0:T(8,128)S(1)}, u32[]{:S(2)}, u32[]{:S(2)}) collective-permute-start(f32[640,256]{1,0:T(8,128)S(1)} %fusion.31), channel_id=1, source_target_pairs={{4,0},{8,4},{12,8},{16,12},{20,16},{24,20},{28,24},{5,1},{9,5},{13... | collective-permute-start | bytes 1966088 | tf_op jit(solution)/shard_map/ppermute | solution.py:17
  149.6 24.7 %collective-permute-start.14 = (f32[320,640]{1,0:T(8,128)S(1)}, f32[320,640]{1,0:T(8,128)}, u32[]{:S(2)}, u32[]{:S(2)}) collective-permute-start(f32[320,640]{1,0:T(8,128)S(1)} %fusion.21), channel_id=1, source_target_pairs={{0,8},{4,12},{8,16},{12,20},{16,24},{20,28},{1,9},{5,13},{9,17},{1... | collective-permute-start | bytes 2457608 | tf_op jit(solution)/shard_map/ppermute | solution.py:17
  156.4 23.1 %collective-permute-start.15 = (f32[320,640]{1,0:T(8,128)S(1)}, f32[320,640]{1,0:T(8,128)S(1)}, u32[]{:S(2)}, u32[]{:S(2)}) collective-permute-start(f32[320,640]{1,0:T(8,128)S(1)} %fusion.21), channel_id=1, source_target_pairs={{8,0},{12,4},{16,8},{20,12},{24,16},{28,20},{9,1},{13,5},{17,9},{2... | collective-permute-start | bytes 2457608 | tf_op jit(solution)/shard_map/ppermute | solution.py:17
  162.6 27.9 %collective-permute-start.19 = (f32[640,256]{1,0:T(8,128)}, f32[640,256]{1,0:T(8,128)}, u32[]{:S(2)}, u32[]{:S(2)}) collective-permute-start(f32[640,256]{1,0:T(8,128)} %fusion.52), channel_id=1, source_target_pairs={{8,0},{12,4},{16,8},{20,12},{24,16},{28,20},{9,1},{13,5},{17,9},{2... | collective-permute-start | bytes 1966088 | tf_op jit(solution)/shard_map/ppermute | solution.py:17
  163.9 29.1 %collective-permute-start.18 = (f32[640,256]{1,0:T(8,128)}, f32[640,256]{1,0:T(8,128)}, u32[]{:S(2)}, u32[]{:S(2)}) collective-permute-start(f32[640,256]{1,0:T(8,128)} %fusion.52), channel_id=1, source_target_pairs={{0,8},{4,12},{8,16},{12,20},{16,24},{20,28},{1,9},{5,13},{9,17},{1... | collective-permute-start | bytes 1966088 | tf_op jit(solution)/shard_map/ppermute | solution.py:17
  (23 other events, 645.3 us)
Sparse Core Ops, SparseCore 0:
  116.3 20.6 all-gather.2
  139.1 20.0 all-gather.4
